TPU v7x, 128 devices: a whole 4x4x4 slice. The times are simulated.
128 devices in a mesh: dp: 16 (over y_lo, z, core), fsdp: 8 (over y_hi, x).
Axes of the slice: x: 4, y: 4 (y_hi: 2, y_lo: 2; y = y_hi * 2 + y_lo), z: 4, core: 2. Of those that a mesh axis runs over, the one named last changes fastest.
Arguments:
- context: bfloat16 [65536, 1024], P(('dp', 'fsdp')), may hold values from -6 to 6
- residual: bfloat16 [65536, 2048], P(('dp', 'fsdp')), may hold values from -6 to 6
- out_weight: bfloat16 [1024, 2048], P('fsdp'), may hold values from -0.1875 to 0.1875
- norm_gain: float32 [2048], replicated, may hold values from 0.5 to 1.5
- user_vectors: bfloat16 [1024, 2048], P(('dp', 'fsdp')), may hold values from -12 to 12
- positive: int32 [1024], P(('dp', 'fsdp')), may hold values from 0 to 255
- item_ids: int32 [256], P(('dp', 'fsdp')), may hold values from 0 to 127
- item_counts: int32 [256], P(('dp', 'fsdp')), may hold values from 1 to 5000
- lengths: int32 [256], P(('dp', 'fsdp')), may hold values from 64 to 256
Outputs:
- mean_loss: float32 [], replicated
- residual_grad: bfloat16 [65536, 2048], P(('dp', 'fsdp'))
- context_grad: bfloat16 [65536, 1024], P(('dp', 'fsdp'))
- weight_grad: bfloat16 [1024, 2048], P('fsdp')
- norm_gain_grad: float32 [2048], replicated
- user_grad: bfloat16 [1024, 2048], P(('dp', 'fsdp'))
All inputs are finite; a program needn't handle non-finite values.
Results may differ from a plain program's by a relative error of at most 0.015.
Values may be sent and summed in bfloat16 or wider, within the bound.
No kernel may reach another device: no remote copies, remote signals or barrier semaphores. Data moves between devices by JAX's collectives and lax.ppermute only.
A program may use at most 128 MiB of HBM per device.

v0:
```python
import functools

import jax
import jax.numpy as jnp
from jax import lax
from jax.experimental import pallas as pl
from jax.experimental.pallas import tpu as pltpu
from jax.sharding import PartitionSpec as P

EPSILON = 1e-06
MASKED_FILL = -1e30
AXES = ("dp", "fsdp")
F32 = jnp.float32
BF16 = jnp.bfloat16
VMEM = pl.BlockSpec(memory_space=pltpu.VMEM)
SMEM = pl.BlockSpec(memory_space=pltpu.SMEM)
ANY = pl.BlockSpec(memory_space=pl.ANY)
PARAMS = pltpu.CompilerParams(vmem_limit_bytes=56 * 1024 * 1024)
DEVICES = 128
LABELS = 128


def linear(x, y, z, c):
    return ((((y % 2) * 4 + z) * 2 + c) * 2 + y // 2) * 4 + x


def move(value, where):
    perm = []
    for x in range(4):
        for y in range(4):
            for z in range(4):
                for c in range(2):
                    perm.append((linear(x, y, z, c), linear(*where(x, y, z, c))))
    return lax.ppermute(value, AXES, perm)


def shift(value, axis, k):
    if axis == "x":
        return move(value, lambda x, y, z, c: ((x + k) % 4, y, z, c))
    if axis == "y":
        return move(value, lambda x, y, z, c: (x, (y + k) % 4, z, c))
    return move(value, lambda x, y, z, c: (x, y, (z + k) % 4, c))


def swap_core(value):
    return move(value, lambda x, y, z, c: (x, y, z, 1 - c))


def swap_y_hi(value):
    return move(value, lambda x, y, z, c: (x, 3 - y, z, c))


def swap_y_lo(value):
    return move(value, lambda x, y, z, c: (x, y ^ 1, z, c))


def swap_z(value, bits):
    return move(value, lambda x, y, z, c: (x, y, z ^ bits, c))


def ring(value, axis):
    return [value] + [shift(value, axis, k) for k in (1, 2, 3)]


def put(pieces, at):
    out = jnp.zeros((4,) + pieces[0].shape, pieces[0].dtype)
    for k, piece in enumerate(pieces):
        out = lax.dynamic_update_index_in_dim(out, piece, (at - k) % 4, 0)
    return out


def dot(left, right):
    return jnp.dot(left, right, preferred_element_type=F32)


def contract_rows(left, right):
    return lax.dot_general(left, right, (((0,), (0,)), ((), ())), preferred_element_type=F32)


def contract_last(left, right):
    return lax.dot_general(left, right, (((1,), (1,)), ((), ())), preferred_element_type=F32)


def column_offsets(core, width):
    half, part = width // 2, width // 4
    mine = pl.multiple_of(core * half, half)
    other = pl.multiple_of((1 - core) * half, half)
    return (
        (mine, pl.multiple_of(mine + part, part)),
        (other, pl.multiple_of(other + part, part)),
    )


def forward_kernel(where, lengths, context, residual, gain, *refs):
    a_refs, b_refs = (refs[0:2], refs[2:4]), (refs[4:8], refs[8:12])
    stream, inverse, pooled, embedding = refs[12:]
    tokens, width = residual.shape
    part = width // 4
    head = context.shape[1]
    block = head // 8
    items = lengths.shape[0]
    length = tokens // items
    for side, (first_at, second_at) in enumerate(column_offsets(where[3], width)):
        acc = residual[:, pl.ds(first_at, part)].astype(F32)
        for yrel in range(2):
            acc = acc + dot(
                context[:, yrel * 4 * block : (yrel + 1) * 4 * block],
                a_refs[side][yrel][...].reshape(4 * block, part),
            )
        stream[:, pl.ds(first_at, part)] = acc
        acc = residual[:, pl.ds(second_at, part)].astype(F32)
        for k in range(4):
            columns = jnp.concatenate(
                [
                    context[:, k * block : (k + 1) * block],
                    context[:, (4 + k) * block : (5 + k) * block],
                ],
                axis=1,
            )
            acc = acc + dot(columns, b_refs[side][k][...].reshape(2 * block, part))
        stream[:, pl.ds(second_at, part)] = acc
    for i in range(items):
        rows = stream[i * length : (i + 1) * length, :]
        inv = lax.rsqrt(jnp.mean(rows * rows, axis=-1, keepdims=True) + EPSILON)
        inverse[i * length : (i + 1) * length, :] = inv
        position = lax.broadcasted_iota(jnp.int32, (length, 1), 0)
        kept = jnp.where(position < lengths[i], inv, 0.0)
        total = jnp.sum(rows * kept, axis=0, keepdims=True)
        pool = total * gain[...] / lengths[i].astype(F32)
        pooled[i : i + 1, :] = pool
    pool = pooled[...]
    scale = lax.rsqrt(jnp.mean(pool * pool, axis=-1, keepdims=True) + EPSILON)
    embedding[...] = (pool * scale).astype(BF16)


def loss_kernel(users_here, where, lengths, gain, pooled, *refs):
    user_refs, emb_refs = refs[:8], refs[8:16]
    loss, gain_grad, item_grad, user_grad = refs[16:20]
    users, placed, grads, emb_grads, user_sem, emb_sem = refs[20:]
    x, y, z, core = where[0], where[1], where[2], where[3]
    group, width = emb_refs[0].shape
    chunk = user_refs[0].shape[0]
    items = 8 * group
    items_here = lengths.shape[0]
    people = users.shape[0]
    copies = []
    for n in range(8):
        side, k = n // 4, n % 4
        c = core if side == 0 else 1 - core
        at = c * 4 + (z - k + 4) % 4
        copies.append(
            pltpu.make_async_copy(
                emb_refs[n], placed.at[pl.ds(pl.multiple_of(at * group, group), group)], emb_sem.at[n]
            )
        )
        copies.append(
            pltpu.make_async_copy(
                user_refs[n], users.at[pl.ds(pl.multiple_of(at * chunk, chunk), chunk)], user_sem.at[n]
            )
        )
    for copy in copies:
        copy.start()
    to = lax.broadcasted_iota(jnp.int32, (items, items), 0)
    of = lax.broadcasted_iota(jnp.int32, (items, items), 1)
    per = group // items_here
    to_chip, of_chip = (to // items_here) % per, (of // items_here) % per
    turned = (
        ((y - of_chip // 4 + 4) % 4 == to_chip // 4)
        & ((x - of_chip % 4 + 4) % 4 == to_chip % 4)
        & (to // group == of // group)
        & (to % items_here == of % items_here)
    )
    turn = jnp.where(turned, 1.0, 0.0).astype(BF16)
    for copy in copies:
        copy.wait()
    emb = dot(turn, placed[...]).astype(BF16)
    labels = users[:, width : width + LABELS]
    person = lax.broadcasted_iota(jnp.int32, (people, items), 0)
    item = lax.broadcasted_iota(jnp.int32, (people, items), 1)
    holder = jnp.where(
        person == (item // items_here) * users_here + item % items_here, 1.0, 0.0
    ).astype(BF16)
    item_labels = contract_rows(labels, holder)
    ids = item_labels[1:2, :]
    log_counts = jnp.log(item_labels[2:3, :] * 128.0 + item_labels[3:4, :])
    chip = lax.broadcasted_iota(jnp.int32, (1, items), 1) // items_here
    which = lax.broadcasted_iota(jnp.int32, (1, items), 1) % items_here
    index = linear(chip % 4, (chip // 4) % 4, (chip // 16) % 4, chip // 64) * items_here + which
    index = index.astype(F32)
    positive = labels[:, 0:1].astype(F32)
    onehot = index == positive
    positive_id = jnp.sum(jnp.where(onehot, ids, 0.0), axis=1, keepdims=True)
    excluded = (ids == positive_id) & jnp.logical_not(onehot)
    scores = contract_last(users[:, :width], emb)
    logits = jnp.where(excluded, MASKED_FILL, scores - log_counts)
    row_max = jnp.max(logits, axis=1, keepdims=True)
    weights = jnp.where(excluded, 0.0, jnp.exp(logits - row_max))
    row_total = jnp.sum(weights, axis=1, keepdims=True)
    picked = jnp.sum(jnp.where(onehot, logits, 0.0), axis=1, keepdims=True)
    losses = row_max + jnp.log(row_total) - picked
    loss[...] = jnp.sum(losses, axis=0, keepdims=True) / people
    grad = (weights / row_total - jnp.where(onehot, 1.0, 0.0)).astype(BF16)
    grads[...] = grad.astype(F32)
    here = ((core * 4 + z) * 4 + y) * 4 + x
    own = grads[pl.ds(pl.multiple_of(here * users_here, users_here), users_here), :].astype(BF16)
    user_grad[...] = dot(own, emb).astype(BF16)
    all_grads = contract_rows(grad, users[:, :width])
    emb_grads[...] = all_grads
    emb_float = emb.astype(F32)
    product = emb_float * all_grads
    mean = jnp.mean(product, axis=-1, keepdims=True)
    gain_sum = jnp.sum(product - emb_float * emb_float * mean, axis=0, keepdims=True)
    gain_grad[...] = gain_sum / gain[...]
    first = here * items_here
    near = emb_grads[pl.ds(pl.multiple_of((first // 8) * 8, 8), 8), :]
    line = lax.broadcasted_iota(jnp.int32, (8, 1), 0)
    for i in range(items_here):
        mine = jnp.sum(jnp.where(line == first % 8 + i, near, 0.0), axis=0, keepdims=True)
        pool = pooled[i : i + 1, :]
        scale = lax.rsqrt(jnp.mean(pool * pool, axis=-1, keepdims=True) + EPSILON)
        pool_grad = scale * mine - pool * scale * scale * scale * jnp.mean(
            pool * mine, axis=-1, keepdims=True
        )
        item_grad[i : i + 1, :] = gain[...] * pool_grad / lengths[i].astype(F32)


def residual_kernel(where, lengths, stream, inverse, item_grad, residual_grad, send):
    tokens, width = stream.shape
    half = width // 2
    items = lengths.shape[0]
    length = tokens // items
    for i in range(items):
        span = slice(i * length, (i + 1) * length)
        rows = stream[span, :]
        inv = inverse[span, :]
        position = lax.broadcasted_iota(jnp.int32, (length, 1), 0)
        kept = jnp.where(position < lengths[i], inv, 0.0)
        row = item_grad[i : i + 1, :]
        mean = jnp.mean(rows * row, axis=-1, keepdims=True)
        residual_grad[span, :] = (kept * row - rows * (kept * inv * inv * mean)).astype(BF16)
    send[...] = residual_grad[:, pl.ds(pl.multiple_of((1 - where[3]) * half, half), half)]


def context_kernel(where, residual_grad, *refs):
    a_refs, b_refs = (refs[0:2], refs[2:4]), (refs[4:8], refs[8:12])
    context_grad = refs[12]
    tokens, width = residual_grad.shape
    part = width // 4
    block = context_grad.shape[1] // 8
    offsets = column_offsets(where[3], width)
    firsts = [residual_grad[:, pl.ds(first, part)] for first, _ in offsets]
    seconds = [residual_grad[:, pl.ds(second, part)] for _, second in offsets]
    from_a = []
    for yrel in range(2):
        from_a.append(
            sum(
                contract_last(firsts[side], a_refs[side][yrel][...].reshape(4 * block, part))
                for side in range(2)
            )
        )
    x, y_hi = where[0], where[1] // 2
    for k in range(4):
        from_b = sum(
            contract_last(seconds[side], b_refs[side][k][...].reshape(2 * block, part))
            for side in range(2)
        )
        for yrel in range(2):
            value = (
                from_a[yrel][:, k * block : (k + 1) * block]
                + from_b[:, yrel * block : (yrel + 1) * block]
            )
            y_to = y_hi if yrel == 0 else 1 - y_hi
            at = pl.multiple_of((y_to * 4 + (x - k + 4) % 4) * block, block)
            context_grad[:, pl.ds(at, block)] = value.astype(BF16)


def blocks_kernel(where, own_context, peer_context, residual_grad, peer_grad, *refs):
    tokens, width = residual_grad.shape
    half, part = width // 2, width // 4
    block = own_context.shape[0] // 8
    first_at, second_at = column_offsets(where[3], width)[0]

    def product(yrel, at, peer_at):
        span = slice(yrel * 4 * block, (yrel + 1) * 4 * block)
        return dot(own_context[span, :], residual_grad[:, pl.ds(at, part)]) + dot(
            peer_context[span, :], peer_grad[:, peer_at : peer_at + part]
        )

    if len(refs) == 1:
        refs[0][...] = product(0, first_at, 0)
        return
    first_send, kept = refs[0], refs[1]
    first_send[...] = product(1, first_at, 0).astype(BF16)
    for yrel in range(2):
        both = product(yrel, second_at, part)
        kept[yrel] = both[:block]
        for k in (1, 2, 3):
            refs[1 + k][yrel] = both[k * block : (k + 1) * block].astype(BF16)


def shaped(shape, dtype=F32):
    return jax.ShapeDtypeStruct(shape, dtype)


def on_device(
    context, residual, out_weight, norm_gain, user_vectors, positive, item_ids, item_counts, lengths
):
    tokens, head = context.shape
    width = residual.shape[1]
    items_here = lengths.shape[0]
    users_here = user_vectors.shape[0]
    dp, fsdp = lax.axis_index("dp"), lax.axis_index("fsdp")
    y_lo, z, core = dp // 8, (dp // 2) % 4, dp % 2
    y_hi, x = fsdp // 4, fsdp % 4
    y = y_hi * 2 + y_lo
    where = jnp.stack([x, y, z, core]).astype(jnp.int32)
    half, part = width // 2, width // 4
    rows = out_weight.shape[0]
    gain = norm_gain[None, :]

    mine = lax.dynamic_slice(out_weight, (0, core * half), (rows, half))
    b_own, a_own = mine[:, part:], mine[:, :part]
    b_first = jnp.stack([b_own, swap_y_hi(b_own)])
    a_near = jnp.stack(ring(a_own, "x"))
    b_pieces = ring(b_first, "x")
    a_pieces = [a_near, swap_y_hi(a_near)]
    pieces = a_pieces + [swap_core(p) for p in a_pieces] + b_pieces + [swap_core(p) for p in b_pieces]

    order = [((y_hi + yrel) % 2) * 4 + (x - k) % 4 for yrel in range(2) for k in range(4)]
    turned = jnp.concatenate(
        [lax.dynamic_slice(context, (0, at * rows), (tokens, rows)) for at in order], axis=1
    )
    own_context = turned.T
    peer_context = swap_core(own_context)

    labels = jnp.stack([item_ids, item_counts // 128, item_counts % 128], axis=1)
    labels = jnp.pad(labels, ((0, users_here - items_here), (0, 0)))
    labels = jnp.concatenate([positive[:, None], labels], axis=1)
    labels = jnp.pad(labels, ((0, 0), (0, LABELS - 4))).astype(BF16)
    users = jnp.concatenate([user_vectors, labels], axis=1)
    users = put(ring(users, "x"), x)
    users = put(ring(users, "y"), y)
    users = ring(users.reshape(16 * users_here, width + LABELS), "z")

    stream, inverse, pooled, embedding = pl.pallas_call(
        forward_kernel,
        out_shape=(
            shaped((tokens, width)),
            shaped((tokens, 1)),
            shaped((items_here, width)),
            shaped((items_here, width), BF16),
        ),
        in_specs=[SMEM, SMEM] + [VMEM] * 15,
        out_specs=(VMEM,) * 4,
        compiler_params=PARAMS,
        name="forward",
    )(where, lengths, turned, residual, gain, *pieces)

    *users, embedding = lax.optimization_barrier((*users, embedding))
    users = users + [swap_core(p) for p in users]
    emb = jnp.stack(ring(embedding, "x"))
    emb = jnp.stack(ring(emb, "y")).reshape(16 * items_here, width)
    emb = ring(emb, "z")
    emb = emb + [swap_core(p) for p in emb]

    people = DEVICES * users_here
    items = DEVICES * items_here
    loss, gain_grad, item_grad, user_grad = pl.pallas_call(
        functools.partial(loss_kernel, users_here),
        out_shape=(
            shaped((1, 1)),
            shaped((1, width)),
            shaped((items_here, width)),
            shaped((users_here, width), BF16),
        ),
        in_specs=[SMEM, SMEM, VMEM, VMEM] + [ANY] * 16,
        out_specs=(VMEM,) * 4,
        scratch_shapes=[
            pltpu.VMEM((people, width + LABELS), BF16),
            pltpu.VMEM((items, width), BF16),
            pltpu.VMEM((people, items), F32),
            pltpu.VMEM((items, width), F32),
            pltpu.SemaphoreType.DMA((8,)),
            pltpu.SemaphoreType.DMA((8,)),
        ],
        compiler_params=PARAMS,
        name="loss",
    )(where, lengths, gain, pooled, *users, *emb)

    residual_grad, send = pl.pallas_call(
        residual_kernel,
        out_shape=(shaped((tokens, width), BF16), shaped((tokens, half), BF16)),
        in_specs=[SMEM, SMEM, VMEM, VMEM, VMEM],
        out_specs=(VMEM,) * 2,
        compiler_params=PARAMS,
        name="residual",
    )(where, lengths, stream, inverse, item_grad)
    peer_grad = swap_core(send)
    context_grad = pl.pallas_call(
        context_kernel,
        out_shape=shaped((tokens, head), BF16),
        in_specs=[SMEM] + [VMEM] * 13,
        out_specs=VMEM,
        compiler_params=PARAMS,
        name="context",
    )(where, residual_grad, *pieces)

    operands = (where, own_context, peer_context, residual_grad, peer_grad)
    first_send, second, *second_send = pl.pallas_call(
        blocks_kernel,
        out_shape=(shaped((4 * rows, part), BF16), shaped((2, rows, part)))
        + (shaped((2, rows, part), BF16),) * 3,
        in_specs=[SMEM] + [VMEM] * 4,
        out_specs=(VMEM,) * 5,
        compiler_params=PARAMS,
        name="blocks_sent",
    )(*operands)
    first = pl.pallas_call(
        blocks_kernel,
        out_shape=shaped((4 * rows, part)),
        in_specs=[SMEM] + [VMEM] * 4,
        out_specs=VMEM,
        compiler_params=PARAMS,
        name="blocks_kept",
    )(*operands)

    first = (first + swap_y_hi(first_send).astype(F32)).reshape(4, rows, part)
    for k in (1, 2, 3):
        second = second + shift(second_send[k - 1], "x", 4 - k).astype(F32)
    arrived = [shift(first[k].astype(BF16), "x", 4 - k) for k in (1, 2, 3)]
    second = second[0] + swap_y_hi(second[1].astype(BF16)).astype(F32)
    first = first[0]
    for piece in arrived:
        first = first + piece.astype(F32)
    own = jnp.concatenate([first, second], axis=1)
    for swap in (swap_y_lo, lambda v: swap_z(v, 1), lambda v: swap_z(v, 3)):
        own = lax.reduce_precision(own, 8, 7)
        own = own + swap(own.astype(BF16)).astype(F32)
    own = own.astype(BF16)
    other = swap_core(own)
    weight_grad = jnp.where(
        core == 0, jnp.concatenate([own, other], axis=1), jnp.concatenate([other, own], axis=1)
    )
    return (loss[0, 0], residual_grad, context_grad, weight_grad, gain_grad[0], user_grad)


def solution(mesh):
    placed = (
        P(AXES, None),
        P(AXES, None),
        P("fsdp", None),
        P(),
        P(AXES, None),
        P(AXES),
        P(AXES),
        P(AXES),
        P(AXES),
    )
    return jax.shard_map(
        on_device,
        mesh=mesh,
        in_specs=placed,
        out_specs=(P(), P(AXES, None), P(AXES, None), P("fsdp", None), P(), P(AXES, None)),
        check_vma=False,
    )
```

profile of v0, /device:TPU:1, one launch (start us, length us, event | category | flops | bytes accessed | tf_op | source)
XLA Modules:
  0.0 187.6 jit_solution(7430877825792340253)
XLA Ops:
  2.9 2.0 %collective-permute-start.14 = (bf16[8,2176]{1,0:T(8,128)(2,1)S(1)}, bf16[8,2176]{1,0:T(8,128)(2,1)S(1)}, u32[]{:S(2)}, u32[]{:S(2)}) collective-permute-start(bf16[8,2176]{1,0:T(8,128)(2,1)S(1)} %fusion.7), channel_id=1, source_target_pairs={{0,1},{8,9},{16,17},{24,25},{32,33},{40,41},{48,49},{56,57},{64,65... | collective-permute-start | bytes 104456 | tf_op jit(solution)/shard_map/ppermute | solution.py:34
  4.9 2.5 %collective-permute-start.15 = (bf16[8,2176]{1,0:T(8,128)(2,1)S(1)}, bf16[8,2176]{1,0:T(8,128)(2,1)S(1)}, u32[]{:S(2)}, u32[]{:S(2)}) collective-permute-start(bf16[8,2176]{1,0:T(8,128)(2,1)S(1)} %fusion.7), channel_id=1, source_target_pairs={{0,2},{8,10},{16,18},{24,26},{32,34},{40,42},{48,50},{56,58},{64,6... | collective-permute-start | bytes 104456 | tf_op jit(solution)/shard_map/ppermute | solution.py:34
  7.4 1.2 collective-permute-start.16
  8.5 1.0 constant_dynamic-slice_fusion.1
  9.9 0.9 collective-permute-start.1
  10.8 2.0 %constant_dynamic-slice_fusion.2 = (bf16[512,128]{1,0:T(8,128)(2,1)}, bf16[512,128]{1,0:T(8,128)(2,1)S(1)}, bf16[512,128]{1,0:T(8,128)(2,1)S(1)}, bf16[512,128]{...) fusion(bf16[512,1024]{1,0:T(8,128)(2,1)} %param.9, ...), kind=kLoop, calls=%fused_computation.41 | loop fusion | bytes 2097184 | tf_op jit(solution)/shard_map/dynamic_slice | solution.py:331
  13.5 0.8 copy.29
  15.8 1.7 collective-permute-start.2
  17.5 2.8 %collective-permute-start.6 = (bf16[128,512]{1,0:T(8,128)(2,1)S(1)}, bf16[128,512]{1,0:T(8,128)(2,1)S(1)}, u32[]{:S(2)}, u32[]{:S(2)}) collective-permute-start(bf16[128,512]{1,0:T(8,128)(2,1)S(1)} %get-tuple-element.59), channel_id=1, source_target_pairs={{0,68},{8,76},{16,84},{24,92},{32,100},{40,108},{48,116},{56,124},... | collective-permute-start | bytes 393224 | tf_op jit(solution)/shard_map/ppermute | solution.py:34
  20.5 2.2 %collective-permute-done.6 = bf16[128,512]{1,0:T(8,128)(2,1)S(1)} collective-permute-done((bf16[128,512]{1,0:T(8,128)(2,1)S(1)}, bf16[128,512]{1,0:T(8,128)(2,1)S(1)}, u32[]{:S(2)}, u32[]{:S(2)}) %collective-permute-start.6) | collective-permute-done | bytes 131104 | tf_op jit(solution)/shard_map/ppermute | solution.py:34
  22.7 1.9 %collective-permute-start.18 = (bf16[4,8,2176]{2,1,0:T(8,128)(2,1)S(1)}, bf16[4,8,2176]{2,1,0:T(8,128)(2,1)S(1)}, u32[]{:S(2)}, u32[]{:S(2)}) collective-permute-start(bf16[4,8,2176]{2,1,0:T(8,128)(2,1)S(1)} %bitcast_dynamic-update-slice_fusion.4), channel_id=1, source_target_pairs={{0,4},{8,12},{16,20},{24,28},{32,36},{40,44},{48,52},{56,60},{64,6... | collective-permute-start | bytes 417800 | tf_op jit(solution)/shard_map/ppermute | solution.py:34
  24.7 0.8 collective-permute-start.19
  26.0 1.9 %collective-permute-start.8 = (bf16[2,128,512]{2,1,0:T(8,128)(2,1)S(1)}, bf16[2,128,512]{2,1,0:T(8,128)(2,1)S(1)}, u32[]{:S(2)}, u32[]{:S(2)}) collective-permute-start(bf16[2,128,512]{2,1,0:T(8,128)(2,1)S(1)} %pad_maximum_fusion.1.refs_4_), channel_id=1, source_target_pairs={{0,2},{8,10},{16,18},{24,26},{32,34},{40,42},{48,50},{56,58},{64,6... | collective-permute-start | bytes 786440 | tf_op jit(solution)/shard_map/ppermute | solution.py:34
  28.0 2.1 %collective-permute-start.9 = (bf16[2,128,512]{2,1,0:T(8,128)(2,1)S(1)}, bf16[2,128,512]{2,1,0:T(8,128)(2,1)}, u32[]{:S(2)}, u32[]{:S(2)}) collective-permute-start(bf16[2,128,512]{2,1,0:T(8,128)(2,1)S(1)} %pad_maximum_fusion.1.refs_4_), channel_id=1, source_target_pairs={{0,3},{8,11},{16,19},{24,27},{32,35},{40,43},{48,51},{56,59},{64,6... | collective-permute-start | bytes 786440 | tf_op jit(solution)/shard_map/ppermute | solution.py:34
  30.0 0.8 collective-permute-start.3
  30.9 6.6 %collective-permute-start.4 = (bf16[4,128,512]{2,1,0:T(8,128)(2,1)S(1)}, bf16[4,128,512]{2,1,0:T(8,128)(2,1)S(1)}, u32[]{:S(2)}, u32[]{:S(2)}) collective-permute-start(bf16[4,128,512]{2,1,0:T(8,128)(2,1)S(1)} %pad_maximum_fusion.refs_0_), channel_id=1, source_target_pairs={{0,8},{8,0},{16,24},{24,16},{32,40},{40,32},{48,56},{56,48},{64,72... | collective-permute-start | bytes 1572872 | tf_op jit(solution)/shard_map/ppermute | solution.py:34
  37.5 3.6 %collective-permute-start.10 = (bf16[2,128,512]{2,1,0:T(8,128)(2,1)S(1)}, bf16[2,128,512]{2,1,0:T(8,128)(2,1)S(1)}, u32[]{:S(2)}, u32[]{:S(2)}) collective-permute-start(bf16[2,128,512]{2,1,0:T(8,128)(2,1)S(1)} %pad_maximum_fusion.1.refs_4_), channel_id=1, source_target_pairs={{0,8},{8,0},{16,24},{24,16},{32,40},{40,32},{48,56},{56,48},{64,72... | collective-permute-start | bytes 786440 | tf_op jit(solution)/shard_map/ppermute | solution.py:34
  42.3 1.6 collective-permute-start.20
  43.9 3.3 %collective-permute-start.21 = (bf16[128,2176]{1,0:T(8,128)(2,1)S(1)}, bf16[128,2176]{1,0:T(8,128)(2,1)}, u32[]{:S(2)}, u32[]{:S(2)}) collective-permute-start(bf16[128,2176]{1,0:T(8,128)(2,1)S(1)} %bitcast.58), channel_id=1, source_target_pairs={{0,32},{8,40},{16,48},{24,56},{32,0},{40,8},{48,16},{56,24},{64,96... | collective-permute-start | bytes 1671176 | tf_op jit(solution)/shard_map/ppermute | solution.py:34
  47.9 2.3 %collective-permute-start.5 = (bf16[4,128,512]{2,1,0:T(8,128)(2,1)S(1)}, bf16[4,128,512]{2,1,0:T(8,128)(2,1)}, u32[]{:S(2)}, u32[]{:S(2)}) collective-permute-start(bf16[4,128,512]{2,1,0:T(8,128)(2,1)S(1)} %collective-permute-done.3.refs_1_), channel_id=1, source_target_pairs={{0,8},{8,0},{16,24},{24,16},{32,40},{40,32},{48,56},{56,48},{64,72... | collective-permute-start | bytes 1572872 | tf_op jit(solution)/shard_map/ppermute | solution.py:34
  51.1 1.7 copy.32
  52.8 0.9 constant_dynamic-update-slice_fusion
  53.7 1.3 copy.23.context
  55.7 7.5 %forward.1 = (f32[512,2048]{1,0:T(8,128)}, f32[512,1]{1,0:T(8,128)}, f32[2,2048]{1,0:T(2,128)}, bf16[2,2048]{1,0:T(2,128)(2,1)}) custom-call(s32[4]{0:T(128)} %pad_add_fusion.where, s32[2]{0:T(128)} %lengths.5, bf16[512,1024]{1,0:T(8,128)(2,1)} %copy.23.context, bf16[512,2048]{1,0:T(8,128)(2,1)} %residual.2, f32[1,2048]{1,0:T(1,128)} %bitcast.68, ...), custom_call_target="tpu_custom_call" | custom-call | tf_op jit(solution)/shard_map/forward/pallas_call | solution.py:345
  63.2 8.4 %collective-permute-done.21.refs_2_ = bf16[128,2176]{1,0:T(8,128)(2,1)} collective-permute-done((bf16[128,2176]{1,0:T(8,128)(2,1)S(1)}, bf16[128,2176]{1,0:T(8,128)(2,1)}, u32[]{:S(2)}, u32[]{:S(2)}) %collective-permute-start.21) | collective-permute-done | bytes 557088 | tf_op jit(solution)/shard_map/ppermute | solution.py:34
  71.6 1.7 collective-permute-start.27
  73.3 1.9 %collective-permute-start.28 = (bf16[2,2048]{1,0:T(2,128)(2,1)}, bf16[2,2048]{1,0:T(2,128)(2,1)S(1)}, u32[]{:S(2)}, u32[]{:S(2)}) collective-permute-start(bf16[2,2048]{1,0:T(2,128)(2,1)} %get-tuple-element.32), channel_id=1, source_target_pairs={{0,2},{8,10},{16,18},{24,26},{32,34},{40,42},{48,50},{56,58},{64,6... | collective-permute-start | bytes 24584 | tf_op jit(solution)/shard_map/ppermute | solution.py:34
  75.2 0.8 collective-permute-start.29
  76.1 1.4 collective-permute-done.28
  79.5 1.7 collective-permute-start.31
  81.2 2.0 %collective-permute-start.32 = (bf16[4,2,2048]{2,1,0:T(2,128)(2,1)S(1)}, bf16[4,2,2048]{2,1,0:T(2,128)(2,1)S(1)}, u32[]{:S(2)}, u32[]{:S(2)}) collective-permute-start(bf16[4,2,2048]{2,1,0:T(2,128)(2,1)S(1)} %pad_maximum_fusion.3), channel_id=1, source_target_pairs={{0,68},{8,76},{16,84},{24,92},{32,100},{40,108},{48,116},{56,124},... | collective-permute-start | bytes 98312 | tf_op jit(solution)/shard_map/ppermute | solution.py:34
  84.5 1.4 collective-permute-start.33
  85.9 2.4 %collective-permute-start.34 = (bf16[32,2048]{1,0:T(8,128)(2,1)S(1)}, bf16[32,2048]{1,0:T(8,128)(2,1)S(1)}, u32[]{:S(2)}, u32[]{:S(2)}) collective-permute-start(bf16[32,2048]{1,0:T(8,128)(2,1)S(1)} %reshape.29.refs_8_), channel_id=1, source_target_pairs={{0,32},{8,40},{16,48},{24,56},{32,0},{40,8},{48,16},{56,24},{64,96... | collective-permute-start | bytes 393224 | tf_op jit(solution)/shard_map/ppermute | solution.py:34
  88.4 5.0 %collective-permute-start.23 = (bf16[128,2176]{1,0:T(8,128)(2,1)S(1)}, bf16[128,2176]{1,0:T(8,128)(2,1)S(1)}, u32[]{:S(2)}, u32[]{:S(2)}) collective-permute-start(bf16[128,2176]{1,0:T(8,128)(2,1)S(1)} %bitcast.60), channel_id=1, source_target_pairs={{0,8},{8,0},{16,24},{24,16},{32,40},{40,32},{48,56},{56,48},{64,72... | collective-permute-start | bytes 1671176 | tf_op jit(solution)/shard_map/ppermute | solution.py:34
  93.4 1.3 collective-permute-start.25
  94.7 1.8 collective-permute-start.26
  97.1 1.1 collective-permute-done.36.refs_12_
  98.6 1.0 collective-permute-done.37.refs_13_
  100.0 1.0 collective-permute-done.38.refs_14_
  101.3 1.0 collective-permute-done.39.refs_15_
  104.1 10.0 %loss.1 = (f32[1,1]{1,0:T(1,128)}, f32[1,2048]{1,0:T(1,128)}, f32[2,2048]{1,0:T(2,128)}, bf16[8,2048]{1,0:T(8,128)(2,1)}) custom-call(s32[4]{0:T(128)} %pad_add_fusion.where, s32[2]{0:T(128)} %lengths.5, f32[1,2048]{1,0:T(1,128)} %bitcast.69, f32[2,2048]{1,0:T(2,128)} %get-tuple-element.26.pooled, bf16[128,2176]{1,0:T(8,128)(2,1)} %bitcast.61, ...), custom_call_target="tpu_custom_call" | custom-call | tf_op jit(solution)/shard_map/loss/pallas_call | solution.py:368
  114.1 4.9 %residual.3 = (bf16[512,2048]{1,0:T(8,128)(2,1)}, bf16[512,1024]{1,0:T(8,128)(2,1)}) custom-call(s32[4]{0:T(128)} %pad_add_fusion.where, s32[2]{0:T(128)} %lengths.5, f32[512,2048]{1,0:T(8,128)} %get-tuple-element.34.stream, f32[512,1]{1,0:T(8,128)} %get-tuple-element.35.inverse, f32[2,2048]{1,0:T(2,128)} %get-tuple-element.36.item_grad), custom_call_target="tpu_custom_call" | custom-call | tf_op jit(solution)/shard_map/residual/pallas_call | solution.py:390
  119.2 2.7 %collective-permute-done.41.peer_grad = bf16[512,1024]{1,0:T(8,128)(2,1)S(1)} collective-permute-done((bf16[512,1024]{1,0:T(8,128)(2,1)}, bf16[512,1024]{1,0:T(8,128)(2,1)S(1)}, u32[]{:S(2)}, u32[]{:S(2)}) %collective-permute-start.41) | collective-permute-done | bytes 1048608 | tf_op jit(solution)/shard_map/ppermute | solution.py:34
  121.9 1.0 copy-done.4
  122.8 5.2 %blocks_sent.1 = (bf16[512,512]{1,0:T(8,128)(2,1)}, f32[2,128,512]{2,1,0:T(8,128)}, bf16[2,128,512]{2,1,0:T(8,128)(2,1)}, bf16[2,128,512]{2,1,0:T(8,128)(2,1)}, bf16[2,128,512]{2,1,0:T(8,128)(2,1)}) custom-call(s32[4]{0:T(128)} %pad_add_fusion.where, bf16[1024,512]{1,0:T(8,128)(2,1)} %bitcast.55, bf16[1024,512]{1,0:T(8,128)(2,1)} %copy-done.3, ...), custom_call_target="tpu_custom_call" | custom-call | tf_op jit(solution)/shard_map/blocks_sent/pallas_call | solution.py:409
  128.1 2.8 %collective-permute-start.46 = (bf16[2,128,512]{2,1,0:T(8,128)(2,1)}, bf16[2,128,512]{2,1,0:T(8,128)(2,1)S(1)}, u32[]{:S(2)}, u32[]{:S(2)}) collective-permute-start(bf16[2,128,512]{2,1,0:T(8,128)(2,1)} %get-tuple-element.41), channel_id=1, source_target_pairs={{0,3},{8,11},{16,19},{24,27},{32,35},{40,43},{48,51},{56,59},{64,6... | collective-permute-start | bytes 786440 | tf_op jit(solution)/shard_map/ppermute | solution.py:34
  131.4 2.5 %collective-permute-start.42 = (bf16[512,512]{1,0:T(8,128)(2,1)}, bf16[512,512]{1,0:T(8,128)(2,1)S(1)}, u32[]{:S(2)}, u32[]{:S(2)}) collective-permute-start(bf16[512,512]{1,0:T(8,128)(2,1)} %get-tuple-element.39), channel_id=1, source_target_pairs={{0,68},{8,76},{16,84},{24,92},{32,100},{40,108},{48,116},{56,124},... | collective-permute-start | bytes 1572872 | tf_op jit(solution)/shard_map/ppermute | solution.py:34
  133.9 4.2 %blocks_kept.1 = f32[512,512]{1,0:T(8,128)} custom-call(s32[4]{0:T(128)} %pad_add_fusion.where, bf16[1024,512]{1,0:T(8,128)(2,1)} %bitcast.56, bf16[1024,512]{1,0:T(8,128)(2,1)} %copy-done.3, bf16[512,2048]{1,0:T(8,128)(2,1)} %get-tuple-element.21.residual_grad, bf16[512,1024]{1,0:T(8,128)(2,1)} %copy-done.4), custom_call_target="tpu_custom_call" | custom-call | tf_op jit(solution)/shard_map/blocks_kept/pallas_call | solution.py:418
  138.1 4.1 %collective-permute-done.46 = bf16[2,128,512]{2,1,0:T(8,128)(2,1)S(1)} collective-permute-done((bf16[2,128,512]{2,1,0:T(8,128)(2,1)}, bf16[2,128,512]{2,1,0:T(8,128)(2,1)S(1)}, u32[]{:S(2)}, u32[]{:S(2)}) %collective-permute-start.46) | collective-permute-done | bytes 262176 | tf_op jit(solution)/shard_map/ppermute | solution.py:34
  142.2 3.6 %collective-permute-done.48 = bf16[2,128,512]{2,1,0:T(8,128)(2,1)S(1)} collective-permute-done((bf16[2,128,512]{2,1,0:T(8,128)(2,1)}, bf16[2,128,512]{2,1,0:T(8,128)(2,1)S(1)}, u32[]{:S(2)}, u32[]{:S(2)}) %collective-permute-start.48) | collective-permute-done | bytes 262176 | tf_op jit(solution)/shard_map/ppermute | solution.py:34
  146.0 2.6 %collective-permute-start.49 = (bf16[128,512]{1,0:T(8,128)(2,1)S(1)}, bf16[128,512]{1,0:T(8,128)(2,1)S(1)}, u32[]{:S(2)}, u32[]{:S(2)}) collective-permute-start(bf16[128,512]{1,0:T(8,128)(2,1)S(1)} %fusion.5), channel_id=1, source_target_pairs={{0,68},{8,76},{16,84},{24,92},{32,100},{40,108},{48,116},{56,124},... | collective-permute-start | bytes 393224 | tf_op jit(solution)/shard_map/ppermute | solution.py:34
  149.6 0.8 collective-permute-start.45
  150.4 1.2 collective-permute-done.49
  151.6 1.2 collective-permute-done.43
  152.8 1.6 collective-permute-done.44
  154.4 2.1 %collective-permute-done.45 = bf16[128,512]{1,0:T(8,128)(2,1)S(1)} collective-permute-done((bf16[128,512]{1,0:T(8,128)(2,1)S(1)}, bf16[128,512]{1,0:T(8,128)(2,1)S(1)}, u32[]{:S(2)}, u32[]{:S(2)}) %collective-permute-start.45) | collective-permute-done | bytes 131104 | tf_op jit(solution)/shard_map/ppermute | solution.py:34
  156.7 5.2 %collective-permute-done.50 = bf16[128,1024]{1,0:T(8,128)(2,1)S(1)} collective-permute-done((bf16[128,1024]{1,0:T(8,128)(2,1)S(1)}, bf16[128,1024]{1,0:T(8,128)(2,1)S(1)}, u32[]{:S(2)}, u32[]{:S(2)}) %collective-permute-start.50) | collective-permute-done | bytes 262176 | tf_op jit(solution)/shard_map/ppermute | solution.py:34
  162.0 1.1 collective-permute-start.51
  163.1 4.2 %collective-permute-done.51 = bf16[128,1024]{1,0:T(8,128)(2,1)S(1)} collective-permute-done((bf16[128,1024]{1,0:T(8,128)(2,1)S(1)}, bf16[128,1024]{1,0:T(8,128)(2,1)S(1)}, u32[]{:S(2)}, u32[]{:S(2)}) %collective-permute-start.51) | collective-permute-done | bytes 262176 | tf_op jit(solution)/shard_map/ppermute | solution.py:34
  167.4 2.2 %collective-permute-start.52 = (bf16[128,1024]{1,0:T(8,128)(2,1)S(1)}, bf16[128,1024]{1,0:T(8,128)(2,1)S(1)}, u32[]{:S(2)}, u32[]{:S(2)}) collective-permute-start(bf16[128,1024]{1,0:T(8,128)(2,1)S(1)} %fusion.1), channel_id=1, source_target_pairs={{0,48},{8,56},{16,32},{24,40},{32,16},{40,24},{48,0},{56,8},{64,11... | collective-permute-start | bytes 786440 | tf_op jit(solution)/shard_map/ppermute | solution.py:34
  169.6 4.3 %collective-permute-done.52 = bf16[128,1024]{1,0:T(8,128)(2,1)S(1)} collective-permute-done((bf16[128,1024]{1,0:T(8,128)(2,1)S(1)}, bf16[128,1024]{1,0:T(8,128)(2,1)S(1)}, u32[]{:S(2)}, u32[]{:S(2)}) %collective-permute-start.52) | collective-permute-done | bytes 262176 | tf_op jit(solution)/shard_map/ppermute | solution.py:34
  174.1 6.2 %collective-permute-start.53 = (bf16[128,1024]{1,0:T(8,128)(2,1)S(1)}, bf16[128,1024]{1,0:T(8,128)(2,1)S(1)}, u32[]{:S(2)}, u32[]{:S(2)}) collective-permute-start(bf16[128,1024]{1,0:T(8,128)(2,1)S(1)} %add_convert_fusion), channel_id=1, source_target_pairs={{0,8},{8,0},{16,24},{24,16},{32,40},{40,32},{48,56},{56,48},{64,72... | collective-permute-start | bytes 786440 | tf_op jit(solution)/shard_map/ppermute | solution.py:34
  180.4 6.3 %context.1 = bf16[512,1024]{1,0:T(8,128)(2,1)} custom-call(s32[4]{0:T(128)} %pad_add_fusion.where, bf16[512,2048]{1,0:T(8,128)(2,1)} %get-tuple-element.21.residual_grad, bf16[4,128,512]{2,1,0:T(8,128)(2,1)} %copy-done.1, bf16[4,128,512]{2,1,0:T(8,128)(2,1)} %copy-done.7, bf16[4,128,512]{2,1,0:T(8,128)(2,1)} %copy-done.8, ...), custom_call_target="tpu_custom_call" | custom-call | tf_op jit(solution)/shard_map/context/pallas_call | solution.py:399
  186.7 0.9 maximum_select_fusion
  (165 shorter events, 17.9 us)
Async XLA Ops:
  2.9 13.0 %collective-permute-start.14 = (bf16[8,2176]{1,0:T(8,128)(2,1)S(1)}, bf16[8,2176]{1,0:T(8,128)(2,1)S(1)}, u32[]{:S(2)}, u32[]{:S(2)}) collective-permute-start(bf16[8,2176]{1,0:T(8,128)(2,1)S(1)} %fusion.7), channel_id=1, source_target_pairs={{0,1},{8,9},{16,17},{24,25},{32,33},{40,41},{48,49},{56,57},{64,65... | collective-permute-start | bytes 104456 | tf_op jit(solution)/shard_map/ppermute | solution.py:34
  4.9 12.6 %collective-permute-start.15 = (bf16[8,2176]{1,0:T(8,128)(2,1)S(1)}, bf16[8,2176]{1,0:T(8,128)(2,1)S(1)}, u32[]{:S(2)}, u32[]{:S(2)}) collective-permute-start(bf16[8,2176]{1,0:T(8,128)(2,1)S(1)} %fusion.7), channel_id=1, source_target_pairs={{0,2},{8,10},{16,18},{24,26},{32,34},{40,42},{48,50},{56,58},{64,6... | collective-permute-start | bytes 104456 | tf_op jit(solution)/shard_map/ppermute | solution.py:34
  7.4 13.0 %collective-permute-start.16 = (bf16[8,2176]{1,0:T(8,128)(2,1)S(1)}, bf16[8,2176]{1,0:T(8,128)(2,1)S(1)}, u32[]{:S(2)}, u32[]{:S(2)}) collective-permute-start(bf16[8,2176]{1,0:T(8,128)(2,1)S(1)} %fusion.7), channel_id=1, source_target_pairs={{0,3},{8,11},{16,19},{24,27},{32,35},{40,43},{48,51},{56,59},{64,6... | collective-permute-start | bytes 104456 | tf_op jit(solution)/shard_map/ppermute | solution.py:34
  9.5 15.2 %collective-permute-start = (bf16[128,512]{1,0:T(8,128)(2,1)S(1)}, bf16[128,512]{1,0:T(8,128)(2,1)S(1)}, u32[]{:S(2)}, u32[]{:S(2)}) collective-permute-start(bf16[128,512]{1,0:T(8,128)(2,1)S(1)} %get-tuple-element.60), channel_id=1, source_target_pairs={{0,1},{8,9},{16,17},{24,25},{32,33},{40,41},{48,49},{56,57},{64,65... | collective-permute-start | bytes 393224 | tf_op jit(solution)/shard_map/ppermute | solution.py:34
  9.9 15.6 %collective-permute-start.1 = (bf16[128,512]{1,0:T(8,128)(2,1)S(1)}, bf16[128,512]{1,0:T(8,128)(2,1)S(1)}, u32[]{:S(2)}, u32[]{:S(2)}) collective-permute-start(bf16[128,512]{1,0:T(8,128)(2,1)S(1)} %get-tuple-element.60), channel_id=1, source_target_pairs={{0,2},{8,10},{16,18},{24,26},{32,34},{40,42},{48,50},{56,58},{64,6... | collective-permute-start | bytes 393224 | tf_op jit(solution)/shard_map/ppermute | solution.py:34
  15.8 34.5 %copy-start.21 = (bf16[512,128]{0,1:T(8,128)(2,1)S(1)}, bf16[512,128]{0,1:T(8,128)(2,1)}, u32[]{:S(2)}) copy-start(bf16[512,128]{0,1:T(8,128)(2,1)} %copy.29) | copy-start | bytes 393220
  15.8 34.5 %copy-start.22 = (bf16[512,128]{0,1:T(8,128)(2,1)S(1)}, bf16[512,128]{0,1:T(8,128)(2,1)}, u32[]{:S(2)}) copy-start(bf16[512,128]{0,1:T(8,128)(2,1)} %copy.30) | copy-start | bytes 393220
  15.8 35.2 %copy-start.20 = (bf16[512,128]{0,1:T(8,128)(2,1)S(1)}, bf16[512,128]{0,1:T(8,128)(2,1)}, u32[]{:S(2)}) copy-start(bf16[512,128]{0,1:T(8,128)(2,1)} %copy.31) | copy-start | bytes 393220
  15.8 10.2 %collective-permute-start.2 = (bf16[128,512]{1,0:T(8,128)(2,1)S(1)}, bf16[128,512]{1,0:T(8,128)(2,1)S(1)}, u32[]{:S(2)}, u32[]{:S(2)}) collective-permute-start(bf16[128,512]{1,0:T(8,128)(2,1)S(1)} %get-tuple-element.60), channel_id=1, source_target_pairs={{0,3},{8,11},{16,19},{24,27},{32,35},{40,43},{48,51},{56,59},{64,6... | collective-permute-start | bytes 393224 | tf_op jit(solution)/shard_map/ppermute | solution.py:34
  17.5 5.2 %collective-permute-start.6 = (bf16[128,512]{1,0:T(8,128)(2,1)S(1)}, bf16[128,512]{1,0:T(8,128)(2,1)S(1)}, u32[]{:S(2)}, u32[]{:S(2)}) collective-permute-start(bf16[128,512]{1,0:T(8,128)(2,1)S(1)} %get-tuple-element.59), channel_id=1, source_target_pairs={{0,68},{8,76},{16,84},{24,92},{32,100},{40,108},{48,116},{56,124},... | collective-permute-start | bytes 393224 | tf_op jit(solution)/shard_map/ppermute | solution.py:34
  20.4 7.6 %collective-permute-start.17 = (bf16[4,8,2176]{2,1,0:T(8,128)(2,1)S(1)}, bf16[4,8,2176]{2,1,0:T(8,128)(2,1)S(1)}, u32[]{:S(2)}, u32[]{:S(2)}) collective-permute-start(bf16[4,8,2176]{2,1,0:T(8,128)(2,1)S(1)} %bitcast_dynamic-update-slice_fusion.4), channel_id=1, source_target_pairs={{0,64},{8,72},{16,80},{24,88},{32,96},{40,104},{48,112},{56,120},{... | collective-permute-start | bytes 417800 | tf_op jit(solution)/shard_map/ppermute | solution.py:34
  22.7 7.3 %collective-permute-start.18 = (bf16[4,8,2176]{2,1,0:T(8,128)(2,1)S(1)}, bf16[4,8,2176]{2,1,0:T(8,128)(2,1)S(1)}, u32[]{:S(2)}, u32[]{:S(2)}) collective-permute-start(bf16[4,8,2176]{2,1,0:T(8,128)(2,1)S(1)} %bitcast_dynamic-update-slice_fusion.4), channel_id=1, source_target_pairs={{0,4},{8,12},{16,20},{24,28},{32,36},{40,44},{48,52},{56,60},{64,6... | collective-permute-start | bytes 417800 | tf_op jit(solution)/shard_map/ppermute | solution.py:34
  24.7 30.4 %copy-start.5 = (bf16[2,128,512]{2,1,0:T(8,128)(2,1)}, bf16[2,128,512]{2,1,0:T(8,128)(2,1)S(1)}, u32[]{:S(2)}) copy-start(bf16[2,128,512]{2,1,0:T(8,128)(2,1)S(1)} %pad_maximum_fusion.1.refs_4_) | copy-start | bytes 786436
  24.7 6.2 %collective-permute-start.19 = (bf16[4,8,2176]{2,1,0:T(8,128)(2,1)S(1)}, bf16[4,8,2176]{2,1,0:T(8,128)(2,1)S(1)}, u32[]{:S(2)}, u32[]{:S(2)}) collective-permute-start(bf16[4,8,2176]{2,1,0:T(8,128)(2,1)S(1)} %bitcast_dynamic-update-slice_fusion.4), channel_id=1, source_target_pairs={{0,68},{8,76},{16,84},{24,92},{32,100},{40,108},{48,116},{56,124},... | collective-permute-start | bytes 417800 | tf_op jit(solution)/shard_map/ppermute | solution.py:34
  25.5 12.0 %collective-permute-start.7 = (bf16[2,128,512]{2,1,0:T(8,128)(2,1)S(1)}, bf16[2,128,512]{2,1,0:T(8,128)(2,1)S(1)}, u32[]{:S(2)}, u32[]{:S(2)}) collective-permute-start(bf16[2,128,512]{2,1,0:T(8,128)(2,1)S(1)} %pad_maximum_fusion.1.refs_4_), channel_id=1, source_target_pairs={{0,1},{8,9},{16,17},{24,25},{32,33},{40,41},{48,49},{56,57},{64,65... | collective-permute-start | bytes 786440 | tf_op jit(solution)/shard_map/ppermute | solution.py:34
  26.0 15.1 %collective-permute-start.8 = (bf16[2,128,512]{2,1,0:T(8,128)(2,1)S(1)}, bf16[2,128,512]{2,1,0:T(8,128)(2,1)S(1)}, u32[]{:S(2)}, u32[]{:S(2)}) collective-permute-start(bf16[2,128,512]{2,1,0:T(8,128)(2,1)S(1)} %pad_maximum_fusion.1.refs_4_), channel_id=1, source_target_pairs={{0,2},{8,10},{16,18},{24,26},{32,34},{40,42},{48,50},{56,58},{64,6... | collective-permute-start | bytes 786440 | tf_op jit(solution)/shard_map/ppermute | solution.py:34
  27.9 27.1 %copy-start.1 = (bf16[4,128,512]{2,1,0:T(8,128)(2,1)}, bf16[4,128,512]{2,1,0:T(8,128)(2,1)S(1)}, u32[]{:S(2)}) copy-start(bf16[4,128,512]{2,1,0:T(8,128)(2,1)S(1)} %pad_maximum_fusion.refs_0_) | copy-start | bytes 1572868
  28.0 13.2 %collective-permute-start.9 = (bf16[2,128,512]{2,1,0:T(8,128)(2,1)S(1)}, bf16[2,128,512]{2,1,0:T(8,128)(2,1)}, u32[]{:S(2)}, u32[]{:S(2)}) collective-permute-start(bf16[2,128,512]{2,1,0:T(8,128)(2,1)S(1)} %pad_maximum_fusion.1.refs_4_), channel_id=1, source_target_pairs={{0,3},{8,11},{16,19},{24,27},{32,35},{40,43},{48,51},{56,59},{64,6... | collective-permute-start | bytes 786440 | tf_op jit(solution)/shard_map/ppermute | solution.py:34
  30.0 13.8 %collective-permute-start.3 = (bf16[4,128,512]{2,1,0:T(8,128)(2,1)S(1)}, bf16[4,128,512]{2,1,0:T(8,128)(2,1)S(1)}, u32[]{:S(2)}, u32[]{:S(2)}) collective-permute-start(bf16[4,128,512]{2,1,0:T(8,128)(2,1)S(1)} %pad_maximum_fusion.refs_0_), channel_id=1, source_target_pairs={{0,68},{8,76},{16,84},{24,92},{32,100},{40,108},{48,116},{56,124},... | collective-permute-start | bytes 1572872 | tf_op jit(solution)/shard_map/ppermute | solution.py:34
  30.9 16.3 %collective-permute-start.4 = (bf16[4,128,512]{2,1,0:T(8,128)(2,1)S(1)}, bf16[4,128,512]{2,1,0:T(8,128)(2,1)S(1)}, u32[]{:S(2)}, u32[]{:S(2)}) collective-permute-start(bf16[4,128,512]{2,1,0:T(8,128)(2,1)S(1)} %pad_maximum_fusion.refs_0_), channel_id=1, source_target_pairs={{0,8},{8,0},{16,24},{24,16},{32,40},{40,32},{48,56},{56,48},{64,72... | collective-permute-start | bytes 1572872 | tf_op jit(solution)/shard_map/ppermute | solution.py:34
  37.5 12.8 %copy-start.9 = (bf16[2,128,512]{2,1,0:T(8,128)(2,1)}, bf16[2,128,512]{2,1,0:T(8,128)(2,1)S(1)}, u32[]{:S(2)}) copy-start(bf16[2,128,512]{2,1,0:T(8,128)(2,1)S(1)} %collective-permute-done.7.refs_5_) | copy-start | bytes 786436
  37.5 4.8 %collective-permute-start.10 = (bf16[2,128,512]{2,1,0:T(8,128)(2,1)S(1)}, bf16[2,128,512]{2,1,0:T(8,128)(2,1)S(1)}, u32[]{:S(2)}, u32[]{:S(2)}) collective-permute-start(bf16[2,128,512]{2,1,0:T(8,128)(2,1)S(1)} %pad_maximum_fusion.1.refs_4_), channel_id=1, source_target_pairs={{0,8},{8,0},{16,24},{24,16},{32,40},{40,32},{48,56},{56,48},{64,72... | collective-permute-start | bytes 786440 | tf_op jit(solution)/shard_map/ppermute | solution.py:34
  41.1 6.8 %collective-permute-start.11 = (bf16[2,128,512]{2,1,0:T(8,128)(2,1)S(1)}, bf16[2,128,512]{2,1,0:T(8,128)(2,1)S(1)}, u32[]{:S(2)}, u32[]{:S(2)}) collective-permute-start(bf16[2,128,512]{2,1,0:T(8,128)(2,1)S(1)} %collective-permute-done.7.refs_5_), channel_id=1, source_target_pairs={{0,8},{8,0},{16,24},{24,16},{32,40},{40,32},{48,56},{56,48},{64,72... | collective-permute-start | bytes 786440 | tf_op jit(solution)/shard_map/ppermute | solution.py:34
  41.2 9.1 %collective-permute-start.12 = (bf16[2,128,512]{2,1,0:T(8,128)(2,1)S(1)}, bf16[2,128,512]{2,1,0:T(8,128)(2,1)S(1)}, u32[]{:S(2)}, u32[]{:S(2)}) collective-permute-start(bf16[2,128,512]{2,1,0:T(8,128)(2,1)S(1)} %collective-permute-done.8.refs_6_), channel_id=1, source_target_pairs={{0,8},{8,0},{16,24},{24,16},{32,40},{40,32},{48,56},{56,48},{64,72... | collective-permute-start | bytes 786440 | tf_op jit(solution)/shard_map/ppermute | solution.py:34
  41.8 46.5 %copy-start.6 = (bf16[4,4,8,2176]{3,2,1,0:T(8,128)(2,1)}, bf16[4,4,8,2176]{3,2,1,0:T(8,128)(2,1)S(1)}, u32[]{:S(2)}) copy-start(bf16[4,4,8,2176]{3,2,1,0:T(8,128)(2,1)S(1)} %bitcast_dynamic-update-slice_fusion) | copy-start | bytes 1671172
  42.3 21.0 %collective-permute-start.20 = (bf16[128,2176]{1,0:T(8,128)(2,1)S(1)}, bf16[128,2176]{1,0:T(8,128)(2,1)}, u32[]{:S(2)}, u32[]{:S(2)}) collective-permute-start(bf16[128,2176]{1,0:T(8,128)(2,1)S(1)} %bitcast.57), channel_id=1, source_target_pairs={{0,16},{8,24},{16,32},{24,40},{32,48},{40,56},{48,0},{56,8},{64,80... | collective-permute-start | bytes 1671176 | tf_op jit(solution)/shard_map/ppermute | solution.py:34
  43.9 27.7 %collective-permute-start.21 = (bf16[128,2176]{1,0:T(8,128)(2,1)S(1)}, bf16[128,2176]{1,0:T(8,128)(2,1)}, u32[]{:S(2)}, u32[]{:S(2)}) collective-permute-start(bf16[128,2176]{1,0:T(8,128)(2,1)S(1)} %bitcast.58), channel_id=1, source_target_pairs={{0,32},{8,40},{16,48},{24,56},{32,0},{40,8},{48,16},{56,24},{64,96... | collective-permute-start | bytes 1671176 | tf_op jit(solution)/shard_map/ppermute | solution.py:34
  47.2 24.4 %collective-permute-start.22 = (bf16[128,2176]{1,0:T(8,128)(2,1)S(1)}, bf16[128,2176]{1,0:T(8,128)(2,1)}, u32[]{:S(2)}, u32[]{:S(2)}) collective-permute-start(bf16[128,2176]{1,0:T(8,128)(2,1)S(1)} %bitcast.59), channel_id=1, source_target_pairs={{0,48},{8,56},{16,0},{24,8},{32,16},{40,24},{48,32},{56,40},{64,11... | collective-permute-start | bytes 1671176 | tf_op jit(solution)/shard_map/ppermute | solution.py:34
  47.9 7.7 %collective-permute-start.5 = (bf16[4,128,512]{2,1,0:T(8,128)(2,1)S(1)}, bf16[4,128,512]{2,1,0:T(8,128)(2,1)}, u32[]{:S(2)}, u32[]{:S(2)}) collective-permute-start(bf16[4,128,512]{2,1,0:T(8,128)(2,1)S(1)} %collective-permute-done.3.refs_1_), channel_id=1, source_target_pairs={{0,8},{8,0},{16,24},{24,16},{32,40},{40,32},{48,56},{56,48},{64,72... | collective-permute-start | bytes 1572872 | tf_op jit(solution)/shard_map/ppermute | solution.py:34
  50.4 5.3 %collective-permute-start.13 = (bf16[2,128,512]{2,1,0:T(8,128)(2,1)}, bf16[2,128,512]{2,1,0:T(8,128)(2,1)}, u32[]{:S(2)}, u32[]{:S(2)}) collective-permute-start(bf16[2,128,512]{2,1,0:T(8,128)(2,1)} %collective-permute-done.9.refs_7_), channel_id=1, source_target_pairs={{0,8},{8,0},{16,24},{24,16},{32,40},{40,32},{48,56},{56,48},{64,72... | collective-permute-start | bytes 786440 | tf_op jit(solution)/shard_map/ppermute | solution.py:34
  53.7 48.6 %copy-start = (bf16[512,1024]{0,1:T(8,128)(2,1)}, bf16[512,1024]{0,1:T(8,128)(2,1)S(1)}, u32[]{:S(2)}) copy-start(bf16[512,1024]{0,1:T(8,128)(2,1)S(1)} %constant_dynamic-update-slice_fusion) | copy-start | bytes 3145732
  71.6 4.5 %collective-permute-start.27 = (bf16[2,2048]{1,0:T(2,128)(2,1)}, bf16[2,2048]{1,0:T(2,128)(2,1)S(1)}, u32[]{:S(2)}, u32[]{:S(2)}) collective-permute-start(bf16[2,2048]{1,0:T(2,128)(2,1)} %get-tuple-element.32), channel_id=1, source_target_pairs={{0,1},{8,9},{16,17},{24,25},{32,33},{40,41},{48,49},{56,57},{64,65... | collective-permute-start | bytes 24584 | tf_op jit(solution)/shard_map/ppermute | solution.py:34
  73.3 4.2 %collective-permute-start.28 = (bf16[2,2048]{1,0:T(2,128)(2,1)}, bf16[2,2048]{1,0:T(2,128)(2,1)S(1)}, u32[]{:S(2)}, u32[]{:S(2)}) collective-permute-start(bf16[2,2048]{1,0:T(2,128)(2,1)} %get-tuple-element.32), channel_id=1, source_target_pairs={{0,2},{8,10},{16,18},{24,26},{32,34},{40,42},{48,50},{56,58},{64,6... | collective-permute-start | bytes 24584 | tf_op jit(solution)/shard_map/ppermute | solution.py:34
  75.2 2.7 %collective-permute-start.29 = (bf16[2,2048]{1,0:T(2,128)(2,1)}, bf16[2,2048]{1,0:T(2,128)(2,1)S(1)}, u32[]{:S(2)}, u32[]{:S(2)}) collective-permute-start(bf16[2,2048]{1,0:T(2,128)(2,1)} %get-tuple-element.32), channel_id=1, source_target_pairs={{0,3},{8,11},{16,19},{24,27},{32,35},{40,43},{48,51},{56,59},{64,6... | collective-permute-start | bytes 24584 | tf_op jit(solution)/shard_map/ppermute | solution.py:34
  78.7 5.2 %collective-permute-start.30 = (bf16[4,2,2048]{2,1,0:T(2,128)(2,1)S(1)}, bf16[4,2,2048]{2,1,0:T(2,128)(2,1)S(1)}, u32[]{:S(2)}, u32[]{:S(2)}) collective-permute-start(bf16[4,2,2048]{2,1,0:T(2,128)(2,1)S(1)} %pad_maximum_fusion.3), channel_id=1, source_target_pairs={{0,64},{8,72},{16,80},{24,88},{32,96},{40,104},{48,112},{56,120},{... | collective-permute-start | bytes 98312 | tf_op jit(solution)/shard_map/ppermute | solution.py:34
  79.5 4.5 %collective-permute-start.31 = (bf16[4,2,2048]{2,1,0:T(2,128)(2,1)S(1)}, bf16[4,2,2048]{2,1,0:T(2,128)(2,1)S(1)}, u32[]{:S(2)}, u32[]{:S(2)}) collective-permute-start(bf16[4,2,2048]{2,1,0:T(2,128)(2,1)S(1)} %pad_maximum_fusion.3), channel_id=1, source_target_pairs={{0,4},{8,12},{16,20},{24,28},{32,36},{40,44},{48,52},{56,60},{64,6... | collective-permute-start | bytes 98312 | tf_op jit(solution)/shard_map/ppermute | solution.py:34
  81.2 3.0 %collective-permute-start.32 = (bf16[4,2,2048]{2,1,0:T(2,128)(2,1)S(1)}, bf16[4,2,2048]{2,1,0:T(2,128)(2,1)S(1)}, u32[]{:S(2)}, u32[]{:S(2)}) collective-permute-start(bf16[4,2,2048]{2,1,0:T(2,128)(2,1)S(1)} %pad_maximum_fusion.3), channel_id=1, source_target_pairs={{0,68},{8,76},{16,84},{24,92},{32,100},{40,108},{48,116},{56,124},... | collective-permute-start | bytes 98312 | tf_op jit(solution)/shard_map/ppermute | solution.py:34
  84.5 18.3 %copy-start.19 = (bf16[32,2048]{1,0:T(8,128)(2,1)}, bf16[32,2048]{1,0:T(8,128)(2,1)S(1)}, u32[]{:S(2)}) copy-start(bf16[32,2048]{1,0:T(8,128)(2,1)S(1)} %reshape.29.refs_8_) | copy-start | bytes 393220
  84.5 8.9 %collective-permute-start.33 = (bf16[32,2048]{1,0:T(8,128)(2,1)S(1)}, bf16[32,2048]{1,0:T(8,128)(2,1)S(1)}, u32[]{:S(2)}, u32[]{:S(2)}) collective-permute-start(bf16[32,2048]{1,0:T(8,128)(2,1)S(1)} %reshape.29.refs_8_), channel_id=1, source_target_pairs={{0,16},{8,24},{16,32},{24,40},{32,48},{40,56},{48,0},{56,8},{64,80... | collective-permute-start | bytes 393224 | tf_op jit(solution)/shard_map/ppermute | solution.py:34
  85.9 8.8 %collective-permute-start.34 = (bf16[32,2048]{1,0:T(8,128)(2,1)S(1)}, bf16[32,2048]{1,0:T(8,128)(2,1)S(1)}, u32[]{:S(2)}, u32[]{:S(2)}) collective-permute-start(bf16[32,2048]{1,0:T(8,128)(2,1)S(1)} %reshape.29.refs_8_), channel_id=1, source_target_pairs={{0,32},{8,40},{16,48},{24,56},{32,0},{40,8},{48,16},{56,24},{64,96... | collective-permute-start | bytes 393224 | tf_op jit(solution)/shard_map/ppermute | solution.py:34
  88.3 8.2 %collective-permute-start.35 = (bf16[32,2048]{1,0:T(8,128)(2,1)S(1)}, bf16[32,2048]{1,0:T(8,128)(2,1)S(1)}, u32[]{:S(2)}, u32[]{:S(2)}) collective-permute-start(bf16[32,2048]{1,0:T(8,128)(2,1)S(1)} %reshape.29.refs_8_), channel_id=1, source_target_pairs={{0,48},{8,56},{16,0},{24,8},{32,16},{40,24},{48,32},{56,40},{64,11... | collective-permute-start | bytes 393224 | tf_op jit(solution)/shard_map/ppermute | solution.py:34
  88.4 14.3 %collective-permute-start.23 = (bf16[128,2176]{1,0:T(8,128)(2,1)S(1)}, bf16[128,2176]{1,0:T(8,128)(2,1)S(1)}, u32[]{:S(2)}, u32[]{:S(2)}) collective-permute-start(bf16[128,2176]{1,0:T(8,128)(2,1)S(1)} %bitcast.60), channel_id=1, source_target_pairs={{0,8},{8,0},{16,24},{24,16},{32,40},{40,32},{48,56},{56,48},{64,72... | collective-permute-start | bytes 1671176 | tf_op jit(solution)/shard_map/ppermute | solution.py:34
  93.4 9.3 %collective-permute-start.24 = (bf16[128,2176]{1,0:T(8,128)(2,1)}, bf16[128,2176]{1,0:T(8,128)(2,1)S(1)}, u32[]{:S(2)}, u32[]{:S(2)}) collective-permute-start(bf16[128,2176]{1,0:T(8,128)(2,1)} %collective-permute-done.20.refs_1_), channel_id=1, source_target_pairs={{0,8},{8,0},{16,24},{24,16},{32,40},{40,32},{48,56},{56,48},{64,72... | collective-permute-start | bytes 1671176 | tf_op jit(solution)/shard_map/ppermute | solution.py:34
  93.4 9.3 %collective-permute-start.25 = (bf16[128,2176]{1,0:T(8,128)(2,1)}, bf16[128,2176]{1,0:T(8,128)(2,1)S(1)}, u32[]{:S(2)}, u32[]{:S(2)}) collective-permute-start(bf16[128,2176]{1,0:T(8,128)(2,1)} %collective-permute-done.21.refs_2_), channel_id=1, source_target_pairs={{0,8},{8,0},{16,24},{24,16},{32,40},{40,32},{48,56},{56,48},{64,72... | collective-permute-start | bytes 1671176 | tf_op jit(solution)/shard_map/ppermute | solution.py:34
  94.7 8.1 %collective-permute-start.26 = (bf16[128,2176]{1,0:T(8,128)(2,1)}, bf16[128,2176]{1,0:T(8,128)(2,1)S(1)}, u32[]{:S(2)}, u32[]{:S(2)}) collective-permute-start(bf16[128,2176]{1,0:T(8,128)(2,1)} %collective-permute-done.22.refs_3_), channel_id=1, source_target_pairs={{0,8},{8,0},{16,24},{24,16},{32,40},{40,32},{48,56},{56,48},{64,72... | collective-permute-start | bytes 1671176 | tf_op jit(solution)/shard_map/ppermute | solution.py:34
  96.5 1.8 collective-permute-start.36
  98.3 1.4 collective-permute-start.37
  99.6 1.3 collective-permute-start.38
  101.0 1.3 collective-permute-start.39
  102.3 16.8 %collective-permute-start.40 = (bf16[1024,512]{1,0:T(8,128)(2,1)S(1)}, bf16[1024,512]{1,0:T(8,128)(2,1)S(1)}, u32[]{:S(2)}, u32[]{:S(2)}) collective-permute-start(bf16[1024,512]{1,0:T(8,128)(2,1)S(1)} %bitcast.54), channel_id=1, source_target_pairs={{0,8},{8,0},{16,24},{24,16},{32,40},{40,32},{48,56},{56,48},{64,72... | collective-permute-start | bytes 3145736 | tf_op jit(solution)/shard_map/ppermute | solution.py:34
  119.0 2.9 %collective-permute-start.41 = (bf16[512,1024]{1,0:T(8,128)(2,1)}, bf16[512,1024]{1,0:T(8,128)(2,1)S(1)}, u32[]{:S(2)}, u32[]{:S(2)}) collective-permute-start(bf16[512,1024]{1,0:T(8,128)(2,1)} %get-tuple-element.38), channel_id=1, source_target_pairs={{0,8},{8,0},{16,24},{24,16},{32,40},{40,32},{48,56},{56,48},{64,72... | collective-permute-start | bytes 3145736 | tf_op jit(solution)/shard_map/ppermute | solution.py:34
  128.1 14.1 %collective-permute-start.46 = (bf16[2,128,512]{2,1,0:T(8,128)(2,1)}, bf16[2,128,512]{2,1,0:T(8,128)(2,1)S(1)}, u32[]{:S(2)}, u32[]{:S(2)}) collective-permute-start(bf16[2,128,512]{2,1,0:T(8,128)(2,1)} %get-tuple-element.41), channel_id=1, source_target_pairs={{0,3},{8,11},{16,19},{24,27},{32,35},{40,43},{48,51},{56,59},{64,6... | collective-permute-start | bytes 786440 | tf_op jit(solution)/shard_map/ppermute | solution.py:34
  130.8 11.3 %collective-permute-start.47 = (bf16[2,128,512]{2,1,0:T(8,128)(2,1)}, bf16[2,128,512]{2,1,0:T(8,128)(2,1)S(1)}, u32[]{:S(2)}, u32[]{:S(2)}) collective-permute-start(bf16[2,128,512]{2,1,0:T(8,128)(2,1)} %get-tuple-element.42), channel_id=1, source_target_pairs={{0,2},{8,10},{16,18},{24,26},{32,34},{40,42},{48,50},{56,58},{64,6... | collective-permute-start | bytes 786440 | tf_op jit(solution)/shard_map/ppermute | solution.py:34
  130.9 15.0 %collective-permute-start.48 = (bf16[2,128,512]{2,1,0:T(8,128)(2,1)}, bf16[2,128,512]{2,1,0:T(8,128)(2,1)S(1)}, u32[]{:S(2)}, u32[]{:S(2)}) collective-permute-start(bf16[2,128,512]{2,1,0:T(8,128)(2,1)} %get-tuple-element.43), channel_id=1, source_target_pairs={{0,1},{8,9},{16,17},{24,25},{32,33},{40,41},{48,49},{56,57},{64,65... | collective-permute-start | bytes 786440 | tf_op jit(solution)/shard_map/ppermute | solution.py:34
  131.4 14.4 %copy-start.18 = (f32[2,128,512]{2,1,0:T(8,128)S(1)}, f32[2,128,512]{2,1,0:T(8,128)}, u32[]{:S(2)}) copy-start(f32[2,128,512]{2,1,0:T(8,128)} %get-tuple-element.40) | copy-start | bytes 1572868
  131.4 17.2 %collective-permute-start.42 = (bf16[512,512]{1,0:T(8,128)(2,1)}, bf16[512,512]{1,0:T(8,128)(2,1)S(1)}, u32[]{:S(2)}, u32[]{:S(2)}) collective-permute-start(bf16[512,512]{1,0:T(8,128)(2,1)} %get-tuple-element.39), channel_id=1, source_target_pairs={{0,68},{8,76},{16,84},{24,92},{32,100},{40,108},{48,116},{56,124},... | collective-permute-start | bytes 1572872 | tf_op jit(solution)/shard_map/ppermute | solution.py:34
  146.0 5.6 %collective-permute-start.49 = (bf16[128,512]{1,0:T(8,128)(2,1)S(1)}, bf16[128,512]{1,0:T(8,128)(2,1)S(1)}, u32[]{:S(2)}, u32[]{:S(2)}) collective-permute-start(bf16[128,512]{1,0:T(8,128)(2,1)S(1)} %fusion.5), channel_id=1, source_target_pairs={{0,68},{8,76},{16,84},{24,92},{32,100},{40,108},{48,116},{56,124},... | collective-permute-start | bytes 393224 | tf_op jit(solution)/shard_map/ppermute | solution.py:34
  148.8 4.0 %collective-permute-start.43 = (bf16[128,512]{1,0:T(8,128)(2,1)S(1)}, bf16[128,512]{1,0:T(8,128)(2,1)S(1)}, u32[]{:S(2)}, u32[]{:S(2)}) collective-permute-start(bf16[128,512]{1,0:T(8,128)(2,1)S(1)} %get-tuple-element.56), channel_id=1, source_target_pairs={{0,3},{8,11},{16,19},{24,27},{32,35},{40,43},{48,51},{56,59},{64,6... | collective-permute-start | bytes 393224 | tf_op jit(solution)/shard_map/ppermute | solution.py:34
  149.0 5.4 %collective-permute-start.44 = (bf16[128,512]{1,0:T(8,128)(2,1)S(1)}, bf16[128,512]{1,0:T(8,128)(2,1)S(1)}, u32[]{:S(2)}, u32[]{:S(2)}) collective-permute-start(bf16[128,512]{1,0:T(8,128)(2,1)S(1)} %get-tuple-element.58), channel_id=1, source_target_pairs={{0,2},{8,10},{16,18},{24,26},{32,34},{40,42},{48,50},{56,58},{64,6... | collective-permute-start | bytes 393224 | tf_op jit(solution)/shard_map/ppermute | solution.py:34
  149.6 7.0 %collective-permute-start.45 = (bf16[128,512]{1,0:T(8,128)(2,1)S(1)}, bf16[128,512]{1,0:T(8,128)(2,1)S(1)}, u32[]{:S(2)}, u32[]{:S(2)}) collective-permute-start(bf16[128,512]{1,0:T(8,128)(2,1)S(1)} %get-tuple-element.57), channel_id=1, source_target_pairs={{0,1},{8,9},{16,17},{24,25},{32,33},{40,41},{48,49},{56,57},{64,65... | collective-permute-start | bytes 393224 | tf_op jit(solution)/shard_map/ppermute | solution.py:34
  156.6 5.3 %collective-permute-start.50 = (bf16[128,1024]{1,0:T(8,128)(2,1)S(1)}, bf16[128,1024]{1,0:T(8,128)(2,1)S(1)}, u32[]{:S(2)}, u32[]{:S(2)}) collective-permute-start(bf16[128,1024]{1,0:T(8,128)(2,1)S(1)} %fusion), channel_id=1, source_target_pairs={{0,64},{8,72},{16,80},{24,88},{32,96},{40,104},{48,112},{56,120},{... | collective-permute-start | bytes 786440 | tf_op jit(solution)/shard_map/ppermute | solution.py:34
  162.0 5.3 %collective-permute-start.51 = (bf16[128,1024]{1,0:T(8,128)(2,1)S(1)}, bf16[128,1024]{1,0:T(8,128)(2,1)S(1)}, u32[]{:S(2)}, u32[]{:S(2)}) collective-permute-start(bf16[128,1024]{1,0:T(8,128)(2,1)S(1)} %fusion.15), channel_id=1, source_target_pairs={{0,16},{8,24},{16,0},{24,8},{32,48},{40,56},{48,32},{56,40},{64,80... | collective-permute-start | bytes 786440 | tf_op jit(solution)/shard_map/ppermute | solution.py:34
  167.4 6.5 %collective-permute-start.52 = (bf16[128,1024]{1,0:T(8,128)(2,1)S(1)}, bf16[128,1024]{1,0:T(8,128)(2,1)S(1)}, u32[]{:S(2)}, u32[]{:S(2)}) collective-permute-start(bf16[128,1024]{1,0:T(8,128)(2,1)S(1)} %fusion.1), channel_id=1, source_target_pairs={{0,48},{8,56},{16,32},{24,40},{32,16},{40,24},{48,0},{56,8},{64,11... | collective-permute-start | bytes 786440 | tf_op jit(solution)/shard_map/ppermute | solution.py:34
  174.1 12.5 %collective-permute-start.53 = (bf16[128,1024]{1,0:T(8,128)(2,1)S(1)}, bf16[128,1024]{1,0:T(8,128)(2,1)S(1)}, u32[]{:S(2)}, u32[]{:S(2)}) collective-permute-start(bf16[128,1024]{1,0:T(8,128)(2,1)S(1)} %add_convert_fusion), channel_id=1, source_target_pairs={{0,8},{8,0},{16,24},{24,16},{32,40},{40,32},{48,56},{56,48},{64,72... | collective-permute-start | bytes 786440 | tf_op jit(solution)/shard_map/ppermute | solution.py:34
  (21 other events, 98.4 us)
where the time goes:
time: 188 us
  starting transfers between devices  81.2 us (43%)
  waiting for transfers between devices  47.6 us (25%)
  Pallas kernels  38.2 us (20%)
  local copies, waits for them, and re-layouts  13 us (7%)
  other arithmetic  6.36 us (3%)
    ppermute x54, starting transfers between devices, move(): return lax.ppermute(value, AXES, perm)  81.2 us
    ppermute x54, waiting for transfers between devices, move(): return lax.ppermute(value, AXES, perm)  47.6 us
    pallas_call x1, Pallas kernels, on_device(): pl.pallas_call(functools.partial(loss_kernel, users_here), out_shape=(sha...  10 us
    pallas_call x1, Pallas kernels, on_device(): pl.pallas_call(forward_kernel, out_shape=(shaped((tokens, width)), shaped...  7.51 us
    unnamed x78, local copies, waits for them, and re-layouts  7.47 us
    pallas_call x1, Pallas kernels, on_device(): pl.pallas_call(context_kernel, out_shape=shaped((tokens, head), BF16), in...  6.3 us
    pallas_call x1, Pallas kernels, on_device(): pl.pallas_call(blocks_kernel, out_shape=(shaped((4 * rows, part), BF16),...  5.24 us
    pallas_call x1, Pallas kernels, on_device(): pl.pallas_call(residual_kernel, out_shape=(shaped((tokens, width), BF16),...  4.92 us
  transfers between devices with their start and end apart: 54, of which 20 were waited for; matrix products, arithmetic and copies ran while one was open for 6% of the time, Pallas kernels for 18%

commit v1 on v0

--- a/solution.py
+++ b/solution.py
@@ -15,7 +15,15 @@
 VMEM = pl.BlockSpec(memory_space=pltpu.VMEM)
 SMEM = pl.BlockSpec(memory_space=pltpu.SMEM)
 ANY = pl.BlockSpec(memory_space=pl.ANY)
-PARAMS = pltpu.CompilerParams(vmem_limit_bytes=56 * 1024 * 1024)
+
+
+def params(mebibytes):
+    return pltpu.CompilerParams(vmem_limit_bytes=mebibytes * 1024 * 1024)
+
+
+def after(value, other):
+    return lax.optimization_barrier((value, other))[0]
+
 DEVICES = 128
 LABELS = 128
 
@@ -320,15 +328,17 @@
 
     mine = lax.dynamic_slice(out_weight, (0, core * half), (rows, half))
     b_own, a_own = mine[:, part:], mine[:, :part]
-    b_first = jnp.stack([b_own, swap_y_hi(b_own)])
+    b_other = swap_y_hi(b_own)
+    b_first = jnp.stack([b_own, b_other])
     a_near = jnp.stack(ring(a_own, "x"))
     b_pieces = ring(b_first, "x")
     a_pieces = [a_near, swap_y_hi(a_near)]
     pieces = a_pieces + [swap_core(p) for p in a_pieces] + b_pieces + [swap_core(p) for p in b_pieces]
 
     order = [((y_hi + yrel) % 2) * 4 + (x - k) % 4 for yrel in range(2) for k in range(4)]
+    later = after(context, b_other)
     turned = jnp.concatenate(
-        [lax.dynamic_slice(context, (0, at * rows), (tokens, rows)) for at in order], axis=1
+        [lax.dynamic_slice(later, (0, at * rows), (tokens, rows)) for at in order], axis=1
     )
     own_context = turned.T
     peer_context = swap_core(own_context)
@@ -337,7 +347,7 @@
     labels = jnp.pad(labels, ((0, users_here - items_here), (0, 0)))
     labels = jnp.concatenate([positive[:, None], labels], axis=1)
     labels = jnp.pad(labels, ((0, 0), (0, LABELS - 4))).astype(BF16)
-    users = jnp.concatenate([user_vectors, labels], axis=1)
+    users = after(jnp.concatenate([user_vectors, labels], axis=1), b_other)
     users = put(ring(users, "x"), x)
     users = put(ring(users, "y"), y)
     users = ring(users.reshape(16 * users_here, width + LABELS), "z")
@@ -352,14 +362,14 @@
         ),
         in_specs=[SMEM, SMEM] + [VMEM] * 15,
         out_specs=(VMEM,) * 4,
-        compiler_params=PARAMS,
+        compiler_params=params(20),
         name="forward",
     )(where, lengths, turned, residual, gain, *pieces)
 
-    *users, embedding = lax.optimization_barrier((*users, embedding))
-    users = users + [swap_core(p) for p in users]
     emb = jnp.stack(ring(embedding, "x"))
     emb = jnp.stack(ring(emb, "y")).reshape(16 * items_here, width)
+    users = after(users, emb)
+    users = users + [swap_core(p) for p in users]
     emb = ring(emb, "z")
     emb = emb + [swap_core(p) for p in emb]
 
@@ -383,7 +393,7 @@
             pltpu.SemaphoreType.DMA((8,)),
             pltpu.SemaphoreType.DMA((8,)),
         ],
-        compiler_params=PARAMS,
+        compiler_params=params(32),
         name="loss",
     )(where, lengths, gain, pooled, *users, *emb)
 
@@ -392,7 +402,7 @@
         out_shape=(shaped((tokens, width), BF16), shaped((tokens, half), BF16)),
         in_specs=[SMEM, SMEM, VMEM, VMEM, VMEM],
         out_specs=(VMEM,) * 2,
-        compiler_params=PARAMS,
+        compiler_params=params(16),
         name="residual",
     )(where, lengths, stream, inverse, item_grad)
     peer_grad = swap_core(send)
@@ -401,7 +411,7 @@
         out_shape=shaped((tokens, head), BF16),
         in_specs=[SMEM] + [VMEM] * 13,
         out_specs=VMEM,
-        compiler_params=PARAMS,
+        compiler_params=params(14),
         name="context",
     )(where, residual_grad, *pieces)
 
@@ -412,7 +422,7 @@
         + (shaped((2, rows, part), BF16),) * 3,
         in_specs=[SMEM] + [VMEM] * 4,
         out_specs=(VMEM,) * 5,
-        compiler_params=PARAMS,
+        compiler_params=params(14),
         name="blocks_sent",
     )(*operands)
     first = pl.pallas_call(
@@ -420,7 +430,7 @@
         out_shape=shaped((4 * rows, part)),
         in_specs=[SMEM] + [VMEM] * 4,
         out_specs=VMEM,
-        compiler_params=PARAMS,
+        compiler_params=params(14),
         name="blocks_kept",
     )(*operands)
 
@@ -433,6 +443,7 @@
     for piece in arrived:
         first = first + piece.astype(F32)
     own = jnp.concatenate([first, second], axis=1)
+    own, context_grad = lax.optimization_barrier((own, context_grad))
     for swap in (swap_y_lo, lambda v: swap_z(v, 1), lambda v: swap_z(v, 3)):
         own = lax.reduce_precision(own, 8, 7)
         own = own + swap(own.astype(BF16)).astype(F32)

time: 188 us -> 185 us (0.984)
  waiting for transfers between devices: 47.6 us -> 71.8 us
  starting transfers between devices: 81.2 us -> 65.2 us
  Pallas kernels: 38.2 us -> 24.8 us
  local copies, waits for them, and re-layouts: 13 us -> 15.7 us
    ppermute x54, waiting for transfers between devices: 47.6 us -> 71.8 us  [move(): return lax.ppermute(value, AXES, perm)]
    ppermute x54, starting transfers between devices: 81.2 us -> 65.2 us  [move(): return lax.ppermute(value, AXES, perm)]
    dynamic_update_slice x7 -> x8, local copies, waits for them, and re-layouts: 0.11 us -> 6.21 us  [put(): out = lax.dynamic_update_index_in_dim(out, piece, (at - k) % 4, 0)]
    pallas_call x1, Pallas kernels: 7.51 us -> 4.18 us  [on_device(): pl.pallas_call(forward_kernel, out_shape=(shaped((tokens, width)), shaped...]
    pallas_call x1, Pallas kernels: 4.19 us -> 1.24 us  [on_device(): pl.pallas_call(blocks_kernel, out_shape=shaped((4 * rows, part)), in_spec...]
    pallas_call x1, Pallas kernels: 5.24 us -> 2.33 us  [on_device(): pl.pallas_call(blocks_kernel, out_shape=(shaped((4 * rows, part), BF16),...]
    dynamic_slice x1 -> x0, local copies, waits for them, and re-layouts: 2.04 us -> none  [on_device(): lax.dynamic_slice(context, (0, at * rows), (tokens, rows))]
    pallas_call x1, Pallas kernels: 4.92 us -> 2.88 us  [on_device(): pl.pallas_call(residual_kernel, out_shape=(shaped((tokens, width), BF16),...]
  transfers between devices with their start and end apart: 54 -> 54, of which waited for: 20 -> 27; matrix products, arithmetic and copies ran while one was open for 6% -> 7% of each run, Pallas kernels for 18% -> 12%
where the time goes in v1:
time: 185 us; the launch traced here: 184 us
  waiting for transfers between devices  71.8 us (39%)
  starting transfers between devices  65.2 us (35%)
  Pallas kernels  24.8 us (13%)
  local copies, waits for them, and re-layouts  15.7 us (8%)
  other arithmetic  5.38 us (3%)
    ppermute x54, waiting for transfers between devices, move(): return lax.ppermute(value, AXES, perm)  71.8 us
    ppermute x54, starting transfers between devices, move(): return lax.ppermute(value, AXES, perm)  65.2 us
    pallas_call x1, Pallas kernels, on_device(): pl.pallas_call(functools.partial(loss_kernel, users_here), out_shape=(sha...  9.52 us
    unnamed x74, local copies, waits for them, and re-layouts  6.38 us
    dynamic_update_slice x8, local copies, waits for them, and re-layouts, put(): out = lax.dynamic_update_index_in_dim(out, piece, (at - k) % 4, 0)  6.21 us
    pallas_call x1, Pallas kernels, on_device(): pl.pallas_call(context_kernel, out_shape=shaped((tokens, head), BF16), in...  4.61 us
    pallas_call x1, Pallas kernels, on_device(): pl.pallas_call(forward_kernel, out_shape=(shaped((tokens, width)), shaped...  4.18 us
  transfers between devices with their start and end apart: 54, of which 27 were waited for; matrix products, arithmetic and copies ran while one was open for 7% of the time, Pallas kernels for 12%

profile of v1, /device:TPU:1, one launch (start us, length us, event | category | flops | bytes accessed | tf_op | source)
XLA Modules:
  0.0 184.3 jit_solution(16665065323459584570)
XLA Ops:
  0.7 1.1 constant_dynamic-slice_fusion.1
  1.8 2.1 %collective-permute-start.1 = (bf16[128,512]{1,0:T(8,128)(2,1)S(1)}, bf16[128,512]{1,0:T(8,128)(2,1)S(1)}, u32[]{:S(2)}, u32[]{:S(2)}) collective-permute-start(bf16[128,512]{1,0:T(8,128)(2,1)S(1)} %get-tuple-element.57), channel_id=1, source_target_pairs={{0,1},{8,9},{16,17},{24,25},{32,33},{40,41},{48,49},{56,57},{64,65... | collective-permute-start | bytes 393224 | tf_op jit(solution)/shard_map/ppermute | solution.py:42
  3.9 2.5 %collective-permute-start.2 = (bf16[128,512]{1,0:T(8,128)(2,1)S(1)}, bf16[128,512]{1,0:T(8,128)(2,1)S(1)}, u32[]{:S(2)}, u32[]{:S(2)}) collective-permute-start(bf16[128,512]{1,0:T(8,128)(2,1)S(1)} %get-tuple-element.57), channel_id=1, source_target_pairs={{0,2},{8,10},{16,18},{24,26},{32,34},{40,42},{48,50},{56,58},{64,6... | collective-permute-start | bytes 393224 | tf_op jit(solution)/shard_map/ppermute | solution.py:42
  6.3 1.2 collective-permute-start.3
  7.5 2.7 %collective-permute-start = (bf16[128,512]{1,0:T(8,128)(2,1)S(1)}, bf16[128,512]{1,0:T(8,128)(2,1)S(1)}, u32[]{:S(2)}, u32[]{:S(2)}) collective-permute-start(bf16[128,512]{1,0:T(8,128)(2,1)S(1)} %get-tuple-element.58), channel_id=1, source_target_pairs={{0,68},{8,76},{16,84},{24,92},{32,100},{40,108},{48,116},{56,124},... | collective-permute-start | bytes 393224 | tf_op jit(solution)/shard_map/ppermute | solution.py:42
  12.8 2.2 %collective-permute-start.4 = (bf16[4,128,512]{2,1,0:T(8,128)(2,1)S(1)}, bf16[4,128,512]{2,1,0:T(8,128)(2,1)S(1)}, u32[]{:S(2)}, u32[]{:S(2)}) collective-permute-start(bf16[4,128,512]{2,1,0:T(8,128)(2,1)S(1)} %pad_maximum_fusion.refs_0_), channel_id=1, source_target_pairs={{0,68},{8,76},{16,84},{24,92},{32,100},{40,108},{48,116},{56,124},... | collective-permute-start | bytes 1572872 | tf_op jit(solution)/shard_map/ppermute | solution.py:42
  14.9 1.8 collective-permute-start.5
  16.8 1.1 collective-permute-start.14
  17.8 2.1 %collective-permute-start.15 = (bf16[8,2176]{1,0:T(8,128)(2,1)S(1)}, bf16[8,2176]{1,0:T(8,128)(2,1)S(1)}, u32[]{:S(2)}, u32[]{:S(2)}) collective-permute-start(bf16[8,2176]{1,0:T(8,128)(2,1)S(1)} %fusion.7), channel_id=1, source_target_pairs={{0,2},{8,10},{16,18},{24,26},{32,34},{40,42},{48,50},{56,58},{64,6... | collective-permute-start | bytes 104456 | tf_op jit(solution)/shard_map/ppermute | solution.py:42
  19.9 1.3 collective-permute-start.16
  21.9 1.0 pad_maximum_fusion.2.refs_4_
  24.5 1.4 bitcast_dynamic-update-slice_fusion.6
  27.1 1.0 collective-permute-start.18
  29.0 1.6 bitcast_dynamic-update-slice_fusion.3
  30.6 5.6 %collective-permute-done.17 = bf16[4,8,2176]{2,1,0:T(8,128)(2,1)S(1)} collective-permute-done((bf16[4,8,2176]{2,1,0:T(8,128)(2,1)}, bf16[4,8,2176]{2,1,0:T(8,128)(2,1)S(1)}, u32[]{:S(2)}, u32[]{:S(2)}) %collective-permute-start.17) | collective-permute-done | bytes 139296 | tf_op jit(solution)/shard_map/ppermute | solution.py:42
  36.2 1.1 collective-permute-start.8
  37.3 1.4 collective-permute-start.9
  38.7 2.0 %collective-permute-start.10 = (bf16[2,128,512]{2,1,0:T(8,128)(2,1)S(1)}, bf16[2,128,512]{2,1,0:T(8,128)(2,1)S(1)}, u32[]{:S(2)}, u32[]{:S(2)}) collective-permute-start(bf16[2,128,512]{2,1,0:T(8,128)(2,1)S(1)} %pad_maximum_fusion.2.refs_4_), channel_id=1, source_target_pairs={{0,8},{8,0},{16,24},{24,16},{32,40},{40,32},{48,56},{56,48},{64,72... | collective-permute-start | bytes 786440 | tf_op jit(solution)/shard_map/ppermute | solution.py:42
  41.3 2.7 %collective-permute-done.8.refs_6_ = bf16[2,128,512]{2,1,0:T(8,128)(2,1)S(1)} collective-permute-done((bf16[2,128,512]{2,1,0:T(8,128)(2,1)S(1)}, bf16[2,128,512]{2,1,0:T(8,128)(2,1)S(1)}, u32[]{:S(2)}, u32[]{:S(2)}) %collective-permute-start.8) | collective-permute-done | bytes 262176 | tf_op jit(solution)/shard_map/ppermute | solution.py:42
  44.1 5.9 %collective-permute-done.9.refs_7_ = bf16[2,128,512]{2,1,0:T(8,128)(2,1)S(1)} collective-permute-done((bf16[2,128,512]{2,1,0:T(8,128)(2,1)S(1)}, bf16[2,128,512]{2,1,0:T(8,128)(2,1)S(1)}, u32[]{:S(2)}, u32[]{:S(2)}) %collective-permute-start.9) | collective-permute-done | bytes 262176 | tf_op jit(solution)/shard_map/ppermute | solution.py:42
  50.0 2.2 %collective-permute-start.11 = (bf16[2,128,512]{2,1,0:T(8,128)(2,1)S(1)}, bf16[2,128,512]{2,1,0:T(8,128)(2,1)S(1)}, u32[]{:S(2)}, u32[]{:S(2)}) collective-permute-start(bf16[2,128,512]{2,1,0:T(8,128)(2,1)S(1)} %collective-permute-done.7.refs_5_), channel_id=1, source_target_pairs={{0,8},{8,0},{16,24},{24,16},{32,40},{40,32},{48,56},{56,48},{64,72... | collective-permute-start | bytes 786440 | tf_op jit(solution)/shard_map/ppermute | solution.py:42
  54.9 1.8 copy-done.6
  56.6 4.2 %forward.1 = (f32[512,2048]{1,0:T(8,128)S(1)}, f32[512,1]{1,0:T(8,128)S(1)}, f32[2,2048]{1,0:T(2,128)S(1)}, bf16[2,2048]{1,0:T(2,128)(2,1)S(1)}) custom-call(s32[4]{0:T(128)S(1)} %pad_add_fusion.where, s32[2]{0:T(128)S(1)} %copy-done.28, bf16[512,1024]{1,0:T(8,128)(2,1)S(1)} %copy.23.context, bf16[512,2048]{1,0:T(8,128)(2,1)S(1)} %copy-done.6, ...), custom_call_target="tpu_custom_call" | custom-call | tf_op jit(solution)/shard_map/forward/pallas_call | solution.py:355
  60.9 2.0 %copy-done.4 = f32[512,2048]{1,0:T(8,128)} copy-done((f32[512,2048]{1,0:T(8,128)}, f32[512,2048]{1,0:T(8,128)S(1)}, u32[]{:S(2)}) %copy-start.4) | copy-done | bytes 4194328
  62.9 3.2 %collective-permute-start.24 = (bf16[2,2048]{1,0:T(2,128)(2,1)S(1)}, bf16[2,2048]{1,0:T(2,128)(2,1)S(1)}, u32[]{:S(2)}, u32[]{:S(2)}) collective-permute-start(bf16[2,2048]{1,0:T(2,128)(2,1)S(1)} %get-tuple-element.32), channel_id=1, source_target_pairs={{0,2},{8,10},{16,18},{24,26},{32,34},{40,42},{48,50},{56,58},{64,6... | collective-permute-start | bytes 24584 | tf_op jit(solution)/shard_map/ppermute | solution.py:42
  66.9 1.6 collective-permute-start.20
  69.0 3.7 %collective-permute-start.21 = (bf16[128,2176]{1,0:T(8,128)(2,1)}, bf16[128,2176]{1,0:T(8,128)(2,1)S(1)}, u32[]{:S(2)}, u32[]{:S(2)}) collective-permute-start(bf16[128,2176]{1,0:T(8,128)(2,1)} %bitcast.23.refs_0_), channel_id=1, source_target_pairs={{0,32},{8,40},{16,48},{24,56},{32,0},{40,8},{48,16},{56,24},{64,96... | collective-permute-start | bytes 1671176 | tf_op jit(solution)/shard_map/ppermute | solution.py:42
  73.3 2.4 %collective-permute-start.28 = (bf16[4,2,2048]{2,1,0:T(2,128)(2,1)S(1)}, bf16[4,2,2048]{2,1,0:T(2,128)(2,1)S(1)}, u32[]{:S(2)}, u32[]{:S(2)}) collective-permute-start(bf16[4,2,2048]{2,1,0:T(2,128)(2,1)S(1)} %pad_maximum_fusion.4), channel_id=1, source_target_pairs={{0,68},{8,76},{16,84},{24,92},{32,100},{40,108},{48,116},{56,124},... | collective-permute-start | bytes 98312 | tf_op jit(solution)/shard_map/ppermute | solution.py:42
  75.8 1.6 collective-permute-done.27
  78.5 1.1 collective-permute-start.33
  79.6 1.7 collective-permute-start.34
  81.3 1.5 collective-permute-done.20.refs_1_
  82.9 1.1 collective-permute-start.35
  84.0 11.7 %collective-permute-done.21.refs_2_ = bf16[128,2176]{1,0:T(8,128)(2,1)S(1)} collective-permute-done((bf16[128,2176]{1,0:T(8,128)(2,1)}, bf16[128,2176]{1,0:T(8,128)(2,1)S(1)}, u32[]{:S(2)}, u32[]{:S(2)}) %collective-permute-start.21) | collective-permute-done | bytes 557088 | tf_op jit(solution)/shard_map/ppermute | solution.py:42
  95.7 3.2 %collective-permute-done.22.refs_3_ = bf16[128,2176]{1,0:T(8,128)(2,1)S(1)} collective-permute-done((bf16[128,2176]{1,0:T(8,128)(2,1)}, bf16[128,2176]{1,0:T(8,128)(2,1)S(1)}, u32[]{:S(2)}, u32[]{:S(2)}) %collective-permute-start.22) | collective-permute-done | bytes 557088 | tf_op jit(solution)/shard_map/ppermute | solution.py:42
  98.9 2.8 %collective-permute-start.29 = (bf16[128,2176]{1,0:T(8,128)(2,1)}, bf16[128,2176]{1,0:T(8,128)(2,1)S(1)}, u32[]{:S(2)}, u32[]{:S(2)}) collective-permute-start(bf16[128,2176]{1,0:T(8,128)(2,1)} %bitcast.23.refs_0_), channel_id=1, source_target_pairs={{0,8},{8,0},{16,24},{24,16},{32,40},{40,32},{48,56},{56,48},{64,72... | collective-permute-start | bytes 1671176 | tf_op jit(solution)/shard_map/ppermute | solution.py:42
  102.3 0.9 collective-permute-start.32
  103.2 1.7 collective-permute-start.36
  104.8 1.1 collective-permute-done.36.refs_12_
  106.3 1.0 collective-permute-done.37.refs_13_
  107.6 1.0 collective-permute-done.38.refs_14_
  109.0 1.0 collective-permute-done.39.refs_15_
  110.4 9.5 %loss.1 = (f32[1,1]{1,0:T(1,128)}, f32[1,2048]{1,0:T(1,128)}, f32[2,2048]{1,0:T(2,128)S(1)}, bf16[8,2048]{1,0:T(8,128)(2,1)}) custom-call(s32[4]{0:T(128)S(1)} %pad_add_fusion.where, s32[2]{0:T(128)S(1)} %copy-done.28, f32[1,2048]{1,0:T(1,128)S(1)} %bitcast.58, f32[2,2048]{1,0:T(2,128)S(1)} %get-tuple-element.30.pooled, bf16[128,2176]{1,0:T(8,128)(2,1)} %bitcast.23.refs_0_, ...), custom_call_target="tpu_custom_call" | custom-call | tf_op jit(solution)/shard_map/loss/pallas_call | solution.py:378
  119.9 2.9 %residual.3 = (bf16[512,2048]{1,0:T(8,128)(2,1)}, bf16[512,1024]{1,0:T(8,128)(2,1)S(1)}) custom-call(s32[4]{0:T(128)S(1)} %pad_add_fusion.where, s32[2]{0:T(128)S(1)} %copy-done.28, f32[512,2048]{1,0:T(8,128)S(1)} %copy-done.5, f32[512,1]{1,0:T(8,128)S(1)} %copy-done.26, f32[2,2048]{1,0:T(2,128)S(1)} %get-tuple-element.40.item_grad), custom_call_target="tpu_custom_call" | custom-call | tf_op jit(solution)/shard_map/residual/pallas_call | solution.py:400
  123.0 2.5 %collective-permute-done.41.peer_grad = bf16[512,1024]{1,0:T(8,128)(2,1)S(1)} collective-permute-done((bf16[512,1024]{1,0:T(8,128)(2,1)S(1)}, bf16[512,1024]{1,0:T(8,128)(2,1)S(1)}, u32[]{:S(2)}, u32[]{:S(2)}) %collective-permute-start.41) | collective-permute-done | bytes 1048608 | tf_op jit(solution)/shard_map/ppermute | solution.py:42
  125.5 1.6 copy-done
  127.1 2.3 %blocks_sent.1 = (bf16[512,512]{1,0:T(8,128)(2,1)S(1)}, f32[2,128,512]{2,1,0:T(8,128)S(1)}, bf16[2,128,512]{2,1,0:T(8,128)(2,1)S(1)}, bf16[2,128,512]{2,1,0:T(8,128)(2,1)S(1)}, bf16[2,128,512]{2,1,0:T(8,128)(2,1)S(1)}) custom-call(s32[4]{0:T(128)S(1)} %pad_add_fusion.where, bf16[1024,512]{1,0:T(8,128)(2,1)S(1)} %bitcast.55, ...), custom_call_target="tpu_custom_call" | custom-call | tf_op jit(solution)/shard_map/blocks_sent/pallas_call | solution.py:419
  129.5 1.2 collective-permute-start.46
  130.6 1.2 collective-permute-start.47
  131.9 2.6 %collective-permute-start.42 = (bf16[512,512]{1,0:T(8,128)(2,1)S(1)}, bf16[512,512]{1,0:T(8,128)(2,1)S(1)}, u32[]{:S(2)}, u32[]{:S(2)}) collective-permute-start(bf16[512,512]{1,0:T(8,128)(2,1)S(1)} %get-tuple-element.43), channel_id=1, source_target_pairs={{0,68},{8,76},{16,84},{24,92},{32,100},{40,108},{48,116},{56,124},... | collective-permute-start | bytes 1572872 | tf_op jit(solution)/shard_map/ppermute | solution.py:42
  134.6 4.6 %context.1 = bf16[512,1024]{1,0:T(8,128)(2,1)} custom-call(s32[4]{0:T(128)S(1)} %pad_add_fusion.where, bf16[512,2048]{1,0:T(8,128)(2,1)S(1)} %copy-done.1, bf16[4,128,512]{2,1,0:T(8,128)(2,1)S(1)} %copy-done.3, bf16[4,128,512]{2,1,0:T(8,128)(2,1)S(1)} %copy-done.8, bf16[4,128,512]{2,1,0:T(8,128)(2,1)} %collective-permute-done.5.refs_2_, ...), custom_call_target="tpu_custom_call" | custom-call | tf_op jit(solution)/shard_map/context/pallas_call | solution.py:409
  139.2 1.2 blocks_kept.1
  140.5 5.5 %collective-permute-done.48 = bf16[2,128,512]{2,1,0:T(8,128)(2,1)S(1)} collective-permute-done((bf16[2,128,512]{2,1,0:T(8,128)(2,1)S(1)}, bf16[2,128,512]{2,1,0:T(8,128)(2,1)S(1)}, u32[]{:S(2)}, u32[]{:S(2)}) %collective-permute-start.48) | collective-permute-done | bytes 262176 | tf_op jit(solution)/shard_map/ppermute | solution.py:42
  146.1 2.8 %collective-permute-start.49 = (bf16[128,512]{1,0:T(8,128)(2,1)S(1)}, bf16[128,512]{1,0:T(8,128)(2,1)S(1)}, u32[]{:S(2)}, u32[]{:S(2)}) collective-permute-start(bf16[128,512]{1,0:T(8,128)(2,1)S(1)} %fusion.4), channel_id=1, source_target_pairs={{0,68},{8,76},{16,84},{24,92},{32,100},{40,108},{48,116},{56,124},... | collective-permute-start | bytes 393224 | tf_op jit(solution)/shard_map/ppermute | solution.py:42
  150.9 1.2 collective-permute-done.49
  152.1 1.4 collective-permute-done.43
  153.5 1.2 collective-permute-done.44
  154.7 3.7 %collective-permute-done.45 = bf16[128,512]{1,0:T(8,128)(2,1)S(1)} collective-permute-done((bf16[128,512]{1,0:T(8,128)(2,1)S(1)}, bf16[128,512]{1,0:T(8,128)(2,1)S(1)}, u32[]{:S(2)}, u32[]{:S(2)}) %collective-permute-start.45) | collective-permute-done | bytes 131104 | tf_op jit(solution)/shard_map/ppermute | solution.py:42
  158.6 6.6 %collective-permute-done.50 = bf16[128,1024]{1,0:T(8,128)(2,1)S(1)} collective-permute-done((bf16[128,1024]{1,0:T(8,128)(2,1)S(1)}, bf16[128,1024]{1,0:T(8,128)(2,1)S(1)}, u32[]{:S(2)}, u32[]{:S(2)}) %collective-permute-start.50) | collective-permute-done | bytes 262176 | tf_op jit(solution)/shard_map/ppermute | solution.py:42
  165.5 5.7 %collective-permute-done.51 = bf16[128,1024]{1,0:T(8,128)(2,1)S(1)} collective-permute-done((bf16[128,1024]{1,0:T(8,128)(2,1)S(1)}, bf16[128,1024]{1,0:T(8,128)(2,1)S(1)}, u32[]{:S(2)}, u32[]{:S(2)}) %collective-permute-start.51) | collective-permute-done | bytes 262176 | tf_op jit(solution)/shard_map/ppermute | solution.py:42
  171.3 2.6 %collective-permute-start.52 = (bf16[128,1024]{1,0:T(8,128)(2,1)S(1)}, bf16[128,1024]{1,0:T(8,128)(2,1)S(1)}, u32[]{:S(2)}, u32[]{:S(2)}) collective-permute-start(bf16[128,1024]{1,0:T(8,128)(2,1)S(1)} %fusion), channel_id=1, source_target_pairs={{0,48},{8,56},{16,32},{24,40},{32,16},{40,24},{48,0},{56,8},{64,11... | collective-permute-start | bytes 786440 | tf_op jit(solution)/shard_map/ppermute | solution.py:42
  173.9 3.9 %collective-permute-done.52 = bf16[128,1024]{1,0:T(8,128)(2,1)S(1)} collective-permute-done((bf16[128,1024]{1,0:T(8,128)(2,1)S(1)}, bf16[128,1024]{1,0:T(8,128)(2,1)S(1)}, u32[]{:S(2)}, u32[]{:S(2)}) %collective-permute-start.52) | collective-permute-done | bytes 262176 | tf_op jit(solution)/shard_map/ppermute | solution.py:42
  178.0 4.2 %collective-permute-start.53 = (bf16[128,1024]{1,0:T(8,128)(2,1)S(1)}, bf16[128,1024]{1,0:T(8,128)(2,1)S(1)}, u32[]{:S(2)}, u32[]{:S(2)}) collective-permute-start(bf16[128,1024]{1,0:T(8,128)(2,1)S(1)} %add_convert_fusion), channel_id=1, source_target_pairs={{0,8},{8,0},{16,24},{24,16},{32,40},{40,32},{48,56},{56,48},{64,72... | collective-permute-start | bytes 786440 | tf_op jit(solution)/shard_map/ppermute | solution.py:42
  182.2 1.2 collective-permute-done.53
  (162 shorter events, 18.9 us)
Async XLA Ops:
  0.6 20.6 %copy-start.29 = (bf16[512,1024]{1,0:T(8,128)(2,1)S(1)}, bf16[512,1024]{1,0:T(8,128)(2,1)}, u32[]{:S(2)}) copy-start(bf16[512,1024]{1,0:T(8,128)(2,1)} %param.9) | copy-start | bytes 3145732
  1.7 20.1 %copy-start.31 = (bf16[128,512]{1,0:T(8,128)(2,1)}, bf16[128,512]{1,0:T(8,128)(2,1)S(1)}, u32[]{:S(2)}) copy-start(bf16[128,512]{1,0:T(8,128)(2,1)S(1)} %get-tuple-element.58) | copy-start | bytes 393220
  1.8 10.9 %collective-permute-start.1 = (bf16[128,512]{1,0:T(8,128)(2,1)S(1)}, bf16[128,512]{1,0:T(8,128)(2,1)S(1)}, u32[]{:S(2)}, u32[]{:S(2)}) collective-permute-start(bf16[128,512]{1,0:T(8,128)(2,1)S(1)} %get-tuple-element.57), channel_id=1, source_target_pairs={{0,1},{8,9},{16,17},{24,25},{32,33},{40,41},{48,49},{56,57},{64,65... | collective-permute-start | bytes 393224 | tf_op jit(solution)/shard_map/ppermute | solution.py:42
  3.9 8.8 %collective-permute-start.2 = (bf16[128,512]{1,0:T(8,128)(2,1)S(1)}, bf16[128,512]{1,0:T(8,128)(2,1)S(1)}, u32[]{:S(2)}, u32[]{:S(2)}) collective-permute-start(bf16[128,512]{1,0:T(8,128)(2,1)S(1)} %get-tuple-element.57), channel_id=1, source_target_pairs={{0,2},{8,10},{16,18},{24,26},{32,34},{40,42},{48,50},{56,58},{64,6... | collective-permute-start | bytes 393224 | tf_op jit(solution)/shard_map/ppermute | solution.py:42
  6.3 6.3 %collective-permute-start.3 = (bf16[128,512]{1,0:T(8,128)(2,1)S(1)}, bf16[128,512]{1,0:T(8,128)(2,1)S(1)}, u32[]{:S(2)}, u32[]{:S(2)}) collective-permute-start(bf16[128,512]{1,0:T(8,128)(2,1)S(1)} %get-tuple-element.57), channel_id=1, source_target_pairs={{0,3},{8,11},{16,19},{24,27},{32,35},{40,43},{48,51},{56,59},{64,6... | collective-permute-start | bytes 393224 | tf_op jit(solution)/shard_map/ppermute | solution.py:42
  7.5 9.3 %collective-permute-start = (bf16[128,512]{1,0:T(8,128)(2,1)S(1)}, bf16[128,512]{1,0:T(8,128)(2,1)S(1)}, u32[]{:S(2)}, u32[]{:S(2)}) collective-permute-start(bf16[128,512]{1,0:T(8,128)(2,1)S(1)} %get-tuple-element.58), channel_id=1, source_target_pairs={{0,68},{8,76},{16,84},{24,92},{32,100},{40,108},{48,116},{56,124},... | collective-permute-start | bytes 393224 | tf_op jit(solution)/shard_map/ppermute | solution.py:42
  12.7 42.1 %copy-start.2 = (bf16[4,128,512]{2,1,0:T(8,128)(2,1)}, bf16[4,128,512]{2,1,0:T(8,128)(2,1)S(1)}, u32[]{:S(2)}) copy-start(bf16[4,128,512]{2,1,0:T(8,128)(2,1)S(1)} %pad_maximum_fusion.refs_0_) | copy-start | bytes 1572868
  12.8 39.5 %collective-permute-start.4 = (bf16[4,128,512]{2,1,0:T(8,128)(2,1)S(1)}, bf16[4,128,512]{2,1,0:T(8,128)(2,1)S(1)}, u32[]{:S(2)}, u32[]{:S(2)}) collective-permute-start(bf16[4,128,512]{2,1,0:T(8,128)(2,1)S(1)} %pad_maximum_fusion.refs_0_), channel_id=1, source_target_pairs={{0,68},{8,76},{16,84},{24,92},{32,100},{40,108},{48,116},{56,124},... | collective-permute-start | bytes 1572872 | tf_op jit(solution)/shard_map/ppermute | solution.py:42
  14.9 37.8 %collective-permute-start.5 = (bf16[4,128,512]{2,1,0:T(8,128)(2,1)S(1)}, bf16[4,128,512]{2,1,0:T(8,128)(2,1)}, u32[]{:S(2)}, u32[]{:S(2)}) collective-permute-start(bf16[4,128,512]{2,1,0:T(8,128)(2,1)S(1)} %pad_maximum_fusion.refs_0_), channel_id=1, source_target_pairs={{0,8},{8,0},{16,24},{24,16},{32,40},{40,32},{48,56},{56,48},{64,72... | collective-permute-start | bytes 1572872 | tf_op jit(solution)/shard_map/ppermute | solution.py:42
  16.8 7.5 %collective-permute-start.14 = (bf16[8,2176]{1,0:T(8,128)(2,1)S(1)}, bf16[8,2176]{1,0:T(8,128)(2,1)}, u32[]{:S(2)}, u32[]{:S(2)}) collective-permute-start(bf16[8,2176]{1,0:T(8,128)(2,1)S(1)} %fusion.7), channel_id=1, source_target_pairs={{0,1},{8,9},{16,17},{24,25},{32,33},{40,41},{48,49},{56,57},{64,65... | collective-permute-start | bytes 104456 | tf_op jit(solution)/shard_map/ppermute | solution.py:42
  17.8 8.1 %collective-permute-start.15 = (bf16[8,2176]{1,0:T(8,128)(2,1)S(1)}, bf16[8,2176]{1,0:T(8,128)(2,1)S(1)}, u32[]{:S(2)}, u32[]{:S(2)}) collective-permute-start(bf16[8,2176]{1,0:T(8,128)(2,1)S(1)} %fusion.7), channel_id=1, source_target_pairs={{0,2},{8,10},{16,18},{24,26},{32,34},{40,42},{48,50},{56,58},{64,6... | collective-permute-start | bytes 104456 | tf_op jit(solution)/shard_map/ppermute | solution.py:42
  19.9 6.6 %collective-permute-start.16 = (bf16[8,2176]{1,0:T(8,128)(2,1)S(1)}, bf16[8,2176]{1,0:T(8,128)(2,1)S(1)}, u32[]{:S(2)}, u32[]{:S(2)}) collective-permute-start(bf16[8,2176]{1,0:T(8,128)(2,1)S(1)} %fusion.7), channel_id=1, source_target_pairs={{0,3},{8,11},{16,19},{24,27},{32,35},{40,43},{48,51},{56,59},{64,6... | collective-permute-start | bytes 104456 | tf_op jit(solution)/shard_map/ppermute | solution.py:42
  22.9 31.9 %copy-start.27 = (f32[2048]{0:T(1024)S(1)}, f32[2048]{0:T(1024)}, u32[]{:S(2)}) copy-start(f32[2048]{0:T(1024)} %param.12) | copy-start | bytes 24580
  23.0 31.9 %copy-start.28 = (s32[2]{0:T(128)S(1)}, s32[2]{0:T(128)}, u32[]{:S(2)}) copy-start(s32[2]{0:T(128)} %lengths.5) | copy-start | bytes 28
  24.2 14.4 %collective-permute-start.7 = (bf16[2,128,512]{2,1,0:T(8,128)(2,1)S(1)}, bf16[2,128,512]{2,1,0:T(8,128)(2,1)S(1)}, u32[]{:S(2)}, u32[]{:S(2)}) collective-permute-start(bf16[2,128,512]{2,1,0:T(8,128)(2,1)S(1)} %pad_maximum_fusion.2.refs_4_), channel_id=1, source_target_pairs={{0,1},{8,9},{16,17},{24,25},{32,33},{40,41},{48,49},{56,57},{64,65... | collective-permute-start | bytes 786440 | tf_op jit(solution)/shard_map/ppermute | solution.py:42
  27.1 9.1 %collective-permute-start.17 = (bf16[4,8,2176]{2,1,0:T(8,128)(2,1)}, bf16[4,8,2176]{2,1,0:T(8,128)(2,1)S(1)}, u32[]{:S(2)}, u32[]{:S(2)}) collective-permute-start(bf16[4,8,2176]{2,1,0:T(8,128)(2,1)} %bitcast_dynamic-update-slice_fusion.4), channel_id=1, source_target_pairs={{0,64},{8,72},{16,80},{24,88},{32,96},{40,104},{48,112},{56,120},{... | collective-permute-start | bytes 417800 | tf_op jit(solution)/shard_map/ppermute | solution.py:42
  27.1 10.2 %collective-permute-start.18 = (bf16[4,8,2176]{2,1,0:T(8,128)(2,1)}, bf16[4,8,2176]{2,1,0:T(8,128)(2,1)S(1)}, u32[]{:S(2)}, u32[]{:S(2)}) collective-permute-start(bf16[4,8,2176]{2,1,0:T(8,128)(2,1)} %bitcast_dynamic-update-slice_fusion.4), channel_id=1, source_target_pairs={{0,4},{8,12},{16,20},{24,28},{32,36},{40,44},{48,52},{56,60},{64,6... | collective-permute-start | bytes 417800 | tf_op jit(solution)/shard_map/ppermute | solution.py:42
  36.2 7.9 %collective-permute-start.8 = (bf16[2,128,512]{2,1,0:T(8,128)(2,1)S(1)}, bf16[2,128,512]{2,1,0:T(8,128)(2,1)S(1)}, u32[]{:S(2)}, u32[]{:S(2)}) collective-permute-start(bf16[2,128,512]{2,1,0:T(8,128)(2,1)S(1)} %pad_maximum_fusion.2.refs_4_), channel_id=1, source_target_pairs={{0,2},{8,10},{16,18},{24,26},{32,34},{40,42},{48,50},{56,58},{64,6... | collective-permute-start | bytes 786440 | tf_op jit(solution)/shard_map/ppermute | solution.py:42
  37.3 12.7 %collective-permute-start.9 = (bf16[2,128,512]{2,1,0:T(8,128)(2,1)S(1)}, bf16[2,128,512]{2,1,0:T(8,128)(2,1)S(1)}, u32[]{:S(2)}, u32[]{:S(2)}) collective-permute-start(bf16[2,128,512]{2,1,0:T(8,128)(2,1)S(1)} %pad_maximum_fusion.2.refs_4_), channel_id=1, source_target_pairs={{0,3},{8,11},{16,19},{24,27},{32,35},{40,43},{48,51},{56,59},{64,6... | collective-permute-start | bytes 786440 | tf_op jit(solution)/shard_map/ppermute | solution.py:42
  38.7 22.1 %copy-start.11 = (bf16[2,128,512]{2,1,0:T(8,128)(2,1)}, bf16[2,128,512]{2,1,0:T(8,128)(2,1)S(1)}, u32[]{:S(2)}) copy-start(bf16[2,128,512]{2,1,0:T(8,128)(2,1)S(1)} %collective-permute-done.7.refs_5_) | copy-start | bytes 786436
  38.7 13.5 %collective-permute-start.10 = (bf16[2,128,512]{2,1,0:T(8,128)(2,1)S(1)}, bf16[2,128,512]{2,1,0:T(8,128)(2,1)S(1)}, u32[]{:S(2)}, u32[]{:S(2)}) collective-permute-start(bf16[2,128,512]{2,1,0:T(8,128)(2,1)S(1)} %pad_maximum_fusion.2.refs_4_), channel_id=1, source_target_pairs={{0,8},{8,0},{16,24},{24,16},{32,40},{40,32},{48,56},{56,48},{64,72... | collective-permute-start | bytes 786440 | tf_op jit(solution)/shard_map/ppermute | solution.py:42
  44.0 16.8 %copy-start.13 = (bf16[2,128,512]{2,1,0:T(8,128)(2,1)}, bf16[2,128,512]{2,1,0:T(8,128)(2,1)S(1)}, u32[]{:S(2)}) copy-start(bf16[2,128,512]{2,1,0:T(8,128)(2,1)S(1)} %collective-permute-done.8.refs_6_) | copy-start | bytes 786436
  44.0 22.1 %collective-permute-start.19 = (bf16[4,8,2176]{2,1,0:T(8,128)(2,1)}, bf16[4,8,2176]{2,1,0:T(8,128)(2,1)S(1)}, u32[]{:S(2)}, u32[]{:S(2)}) collective-permute-start(bf16[4,8,2176]{2,1,0:T(8,128)(2,1)} %bitcast_dynamic-update-slice_fusion.4), channel_id=1, source_target_pairs={{0,68},{8,76},{16,84},{24,92},{32,100},{40,108},{48,116},{56,124},... | collective-permute-start | bytes 417800 | tf_op jit(solution)/shard_map/ppermute | solution.py:42
  50.0 10.9 %copy-start.15 = (bf16[2,128,512]{2,1,0:T(8,128)(2,1)}, bf16[2,128,512]{2,1,0:T(8,128)(2,1)S(1)}, u32[]{:S(2)}) copy-start(bf16[2,128,512]{2,1,0:T(8,128)(2,1)S(1)} %collective-permute-done.9.refs_7_) | copy-start | bytes 786436
  50.0 3.5 %collective-permute-start.11 = (bf16[2,128,512]{2,1,0:T(8,128)(2,1)S(1)}, bf16[2,128,512]{2,1,0:T(8,128)(2,1)S(1)}, u32[]{:S(2)}, u32[]{:S(2)}) collective-permute-start(bf16[2,128,512]{2,1,0:T(8,128)(2,1)S(1)} %collective-permute-done.7.refs_5_), channel_id=1, source_target_pairs={{0,8},{8,0},{16,24},{24,16},{32,40},{40,32},{48,56},{56,48},{64,72... | collective-permute-start | bytes 786440 | tf_op jit(solution)/shard_map/ppermute | solution.py:42
  52.2 1.5 collective-permute-start.12
  52.3 1.8 collective-permute-start.13
  52.7 2.1 %collective-permute-start.6 = (bf16[4,128,512]{2,1,0:T(8,128)(2,1)S(1)}, bf16[4,128,512]{2,1,0:T(8,128)(2,1)S(1)}, u32[]{:S(2)}, u32[]{:S(2)}) collective-permute-start(bf16[4,128,512]{2,1,0:T(8,128)(2,1)S(1)} %collective-permute-done.4.refs_1_), channel_id=1, source_target_pairs={{0,8},{8,0},{16,24},{24,16},{32,40},{40,32},{48,56},{56,48},{64,72... | collective-permute-start | bytes 1572872 | tf_op jit(solution)/shard_map/ppermute | solution.py:42
  62.9 15.3 %copy-start.25 = (f32[512,1]{1,0:T(8,128)}, f32[512,1]{1,0:T(8,128)S(1)}, u32[]{:S(2)}) copy-start(f32[512,1]{1,0:T(8,128)S(1)} %get-tuple-element.39.inverse) | copy-start | bytes 6148
  62.9 5.6 %collective-permute-start.23 = (bf16[2,2048]{1,0:T(2,128)(2,1)S(1)}, bf16[2,2048]{1,0:T(2,128)(2,1)S(1)}, u32[]{:S(2)}, u32[]{:S(2)}) collective-permute-start(bf16[2,2048]{1,0:T(2,128)(2,1)S(1)} %get-tuple-element.32), channel_id=1, source_target_pairs={{0,1},{8,9},{16,17},{24,25},{32,33},{40,41},{48,49},{56,57},{64,65... | collective-permute-start | bytes 24584 | tf_op jit(solution)/shard_map/ppermute | solution.py:42
  62.9 5.6 %collective-permute-start.24 = (bf16[2,2048]{1,0:T(2,128)(2,1)S(1)}, bf16[2,2048]{1,0:T(2,128)(2,1)S(1)}, u32[]{:S(2)}, u32[]{:S(2)}) collective-permute-start(bf16[2,2048]{1,0:T(2,128)(2,1)S(1)} %get-tuple-element.32), channel_id=1, source_target_pairs={{0,2},{8,10},{16,18},{24,26},{32,34},{40,42},{48,50},{56,58},{64,6... | collective-permute-start | bytes 24584 | tf_op jit(solution)/shard_map/ppermute | solution.py:42
  66.2 2.5 %collective-permute-start.25 = (bf16[2,2048]{1,0:T(2,128)(2,1)S(1)}, bf16[2,2048]{1,0:T(2,128)(2,1)S(1)}, u32[]{:S(2)}, u32[]{:S(2)}) collective-permute-start(bf16[2,2048]{1,0:T(2,128)(2,1)S(1)} %get-tuple-element.32), channel_id=1, source_target_pairs={{0,3},{8,11},{16,19},{24,27},{32,35},{40,43},{48,51},{56,59},{64,6... | collective-permute-start | bytes 24584 | tf_op jit(solution)/shard_map/ppermute | solution.py:42
  66.9 16.0 %collective-permute-start.20 = (bf16[128,2176]{1,0:T(8,128)(2,1)}, bf16[128,2176]{1,0:T(8,128)(2,1)S(1)}, u32[]{:S(2)}, u32[]{:S(2)}) collective-permute-start(bf16[128,2176]{1,0:T(8,128)(2,1)} %bitcast.23.refs_0_), channel_id=1, source_target_pairs={{0,16},{8,24},{16,32},{24,40},{32,48},{40,56},{48,0},{56,8},{64,80... | collective-permute-start | bytes 1671176 | tf_op jit(solution)/shard_map/ppermute | solution.py:42
  68.7 4.5 %collective-permute-start.26 = (bf16[4,2,2048]{2,1,0:T(2,128)(2,1)S(1)}, bf16[4,2,2048]{2,1,0:T(2,128)(2,1)S(1)}, u32[]{:S(2)}, u32[]{:S(2)}) collective-permute-start(bf16[4,2,2048]{2,1,0:T(2,128)(2,1)S(1)} %pad_maximum_fusion.4), channel_id=1, source_target_pairs={{0,64},{8,72},{16,80},{24,88},{32,96},{40,104},{48,112},{56,120},{... | collective-permute-start | bytes 98312 | tf_op jit(solution)/shard_map/ppermute | solution.py:42
  69.0 26.7 %collective-permute-start.21 = (bf16[128,2176]{1,0:T(8,128)(2,1)}, bf16[128,2176]{1,0:T(8,128)(2,1)S(1)}, u32[]{:S(2)}, u32[]{:S(2)}) collective-permute-start(bf16[128,2176]{1,0:T(8,128)(2,1)} %bitcast.23.refs_0_), channel_id=1, source_target_pairs={{0,32},{8,40},{16,48},{24,56},{32,0},{40,8},{48,16},{56,24},{64,96... | collective-permute-start | bytes 1671176 | tf_op jit(solution)/shard_map/ppermute | solution.py:42
  72.7 26.3 %collective-permute-start.22 = (bf16[128,2176]{1,0:T(8,128)(2,1)}, bf16[128,2176]{1,0:T(8,128)(2,1)S(1)}, u32[]{:S(2)}, u32[]{:S(2)}) collective-permute-start(bf16[128,2176]{1,0:T(8,128)(2,1)} %bitcast.23.refs_0_), channel_id=1, source_target_pairs={{0,48},{8,56},{16,0},{24,8},{32,16},{40,24},{48,32},{56,40},{64,11... | collective-permute-start | bytes 1671176 | tf_op jit(solution)/shard_map/ppermute | solution.py:42
  73.1 4.3 %collective-permute-start.27 = (bf16[4,2,2048]{2,1,0:T(2,128)(2,1)S(1)}, bf16[4,2,2048]{2,1,0:T(2,128)(2,1)S(1)}, u32[]{:S(2)}, u32[]{:S(2)}) collective-permute-start(bf16[4,2,2048]{2,1,0:T(2,128)(2,1)S(1)} %pad_maximum_fusion.4), channel_id=1, source_target_pairs={{0,4},{8,12},{16,20},{24,28},{32,36},{40,44},{48,52},{56,60},{64,6... | collective-permute-start | bytes 98312 | tf_op jit(solution)/shard_map/ppermute | solution.py:42
  73.3 5.0 %collective-permute-start.28 = (bf16[4,2,2048]{2,1,0:T(2,128)(2,1)S(1)}, bf16[4,2,2048]{2,1,0:T(2,128)(2,1)S(1)}, u32[]{:S(2)}, u32[]{:S(2)}) collective-permute-start(bf16[4,2,2048]{2,1,0:T(2,128)(2,1)S(1)} %pad_maximum_fusion.4), channel_id=1, source_target_pairs={{0,68},{8,76},{16,84},{24,92},{32,100},{40,108},{48,116},{56,124},... | collective-permute-start | bytes 98312 | tf_op jit(solution)/shard_map/ppermute | solution.py:42
  78.5 23.2 %collective-permute-start.33 = (bf16[32,2048]{1,0:T(8,128)(2,1)S(1)}, bf16[32,2048]{1,0:T(8,128)(2,1)S(1)}, u32[]{:S(2)}, u32[]{:S(2)}) collective-permute-start(bf16[32,2048]{1,0:T(8,128)(2,1)S(1)} %reshape.29.refs_8_), channel_id=1, source_target_pairs={{0,16},{8,24},{16,32},{24,40},{32,48},{40,56},{48,0},{56,8},{64,80... | collective-permute-start | bytes 393224 | tf_op jit(solution)/shard_map/ppermute | solution.py:42
  79.6 22.6 %collective-permute-start.34 = (bf16[32,2048]{1,0:T(8,128)(2,1)S(1)}, bf16[32,2048]{1,0:T(8,128)(2,1)S(1)}, u32[]{:S(2)}, u32[]{:S(2)}) collective-permute-start(bf16[32,2048]{1,0:T(8,128)(2,1)S(1)} %reshape.29.refs_8_), channel_id=1, source_target_pairs={{0,32},{8,40},{16,48},{24,56},{32,0},{40,8},{48,16},{56,24},{64,96... | collective-permute-start | bytes 393224 | tf_op jit(solution)/shard_map/ppermute | solution.py:42
  82.9 20.3 %collective-permute-start.35 = (bf16[32,2048]{1,0:T(8,128)(2,1)S(1)}, bf16[32,2048]{1,0:T(8,128)(2,1)S(1)}, u32[]{:S(2)}, u32[]{:S(2)}) collective-permute-start(bf16[32,2048]{1,0:T(8,128)(2,1)S(1)} %reshape.29.refs_8_), channel_id=1, source_target_pairs={{0,48},{8,56},{16,0},{24,8},{32,16},{40,24},{48,32},{56,40},{64,11... | collective-permute-start | bytes 393224 | tf_op jit(solution)/shard_map/ppermute | solution.py:42
  98.9 11.4 %collective-permute-start.29 = (bf16[128,2176]{1,0:T(8,128)(2,1)}, bf16[128,2176]{1,0:T(8,128)(2,1)S(1)}, u32[]{:S(2)}, u32[]{:S(2)}) collective-permute-start(bf16[128,2176]{1,0:T(8,128)(2,1)} %bitcast.23.refs_0_), channel_id=1, source_target_pairs={{0,8},{8,0},{16,24},{24,16},{32,40},{40,32},{48,56},{56,48},{64,72... | collective-permute-start | bytes 1671176 | tf_op jit(solution)/shard_map/ppermute | solution.py:42
  101.7 8.6 %collective-permute-start.30 = (bf16[128,2176]{1,0:T(8,128)(2,1)S(1)}, bf16[128,2176]{1,0:T(8,128)(2,1)S(1)}, u32[]{:S(2)}, u32[]{:S(2)}) collective-permute-start(bf16[128,2176]{1,0:T(8,128)(2,1)S(1)} %collective-permute-done.20.refs_1_), channel_id=1, source_target_pairs={{0,8},{8,0},{16,24},{24,16},{32,40},{40,32},{48,56},{56,48},{64,72... | collective-permute-start | bytes 1671176 | tf_op jit(solution)/shard_map/ppermute | solution.py:42
  101.7 8.6 %collective-permute-start.31 = (bf16[128,2176]{1,0:T(8,128)(2,1)S(1)}, bf16[128,2176]{1,0:T(8,128)(2,1)S(1)}, u32[]{:S(2)}, u32[]{:S(2)}) collective-permute-start(bf16[128,2176]{1,0:T(8,128)(2,1)S(1)} %collective-permute-done.21.refs_2_), channel_id=1, source_target_pairs={{0,8},{8,0},{16,24},{24,16},{32,40},{40,32},{48,56},{56,48},{64,72... | collective-permute-start | bytes 1671176 | tf_op jit(solution)/shard_map/ppermute | solution.py:42
  102.3 8.1 %collective-permute-start.32 = (bf16[128,2176]{1,0:T(8,128)(2,1)S(1)}, bf16[128,2176]{1,0:T(8,128)(2,1)S(1)}, u32[]{:S(2)}, u32[]{:S(2)}) collective-permute-start(bf16[128,2176]{1,0:T(8,128)(2,1)S(1)} %collective-permute-done.22.refs_3_), channel_id=1, source_target_pairs={{0,8},{8,0},{16,24},{24,16},{32,40},{40,32},{48,56},{56,48},{64,72... | collective-permute-start | bytes 1671176 | tf_op jit(solution)/shard_map/ppermute | solution.py:42
  103.2 2.7 %collective-permute-start.36 = (bf16[32,2048]{1,0:T(8,128)(2,1)S(1)}, bf16[32,2048]{1,0:T(8,128)(2,1)S(1)}, u32[]{:S(2)}, u32[]{:S(2)}) collective-permute-start(bf16[32,2048]{1,0:T(8,128)(2,1)S(1)} %reshape.29.refs_8_), channel_id=1, source_target_pairs={{0,8},{8,0},{16,24},{24,16},{32,40},{40,32},{48,56},{56,48},{64,72... | collective-permute-start | bytes 393224 | tf_op jit(solution)/shard_map/ppermute | solution.py:42
  105.9 1.4 collective-permute-start.37
  107.3 1.3 collective-permute-start.38
  108.6 1.3 collective-permute-start.39
  110.0 13.0 %collective-permute-start.40 = (bf16[1024,512]{1,0:T(8,128)(2,1)S(1)}, bf16[1024,512]{1,0:T(8,128)(2,1)S(1)}, u32[]{:S(2)}, u32[]{:S(2)}) collective-permute-start(bf16[1024,512]{1,0:T(8,128)(2,1)S(1)} %bitcast.54), channel_id=1, source_target_pairs={{0,8},{8,0},{16,24},{24,16},{32,40},{40,32},{48,56},{56,48},{64,72... | collective-permute-start | bytes 3145736 | tf_op jit(solution)/shard_map/ppermute | solution.py:42
  119.9 14.6 %copy-start.24 = (bf16[2,128,512]{2,1,0:T(8,128)(2,1)S(1)}, bf16[2,128,512]{2,1,0:T(8,128)(2,1)}, u32[]{:S(2)}) copy-start(bf16[2,128,512]{2,1,0:T(8,128)(2,1)} %copy-done.23) | copy-start | bytes 786436
  122.8 2.7 %collective-permute-start.41 = (bf16[512,1024]{1,0:T(8,128)(2,1)S(1)}, bf16[512,1024]{1,0:T(8,128)(2,1)S(1)}, u32[]{:S(2)}, u32[]{:S(2)}) collective-permute-start(bf16[512,1024]{1,0:T(8,128)(2,1)S(1)} %get-tuple-element.42), channel_id=1, source_target_pairs={{0,8},{8,0},{16,24},{24,16},{32,40},{40,32},{48,56},{56,48},{64,72... | collective-permute-start | bytes 3145736 | tf_op jit(solution)/shard_map/ppermute | solution.py:42
  129.5 11.0 %collective-permute-start.46 = (bf16[2,128,512]{2,1,0:T(8,128)(2,1)S(1)}, bf16[2,128,512]{2,1,0:T(8,128)(2,1)S(1)}, u32[]{:S(2)}, u32[]{:S(2)}) collective-permute-start(bf16[2,128,512]{2,1,0:T(8,128)(2,1)S(1)} %get-tuple-element.45), channel_id=1, source_target_pairs={{0,3},{8,11},{16,19},{24,27},{32,35},{40,43},{48,51},{56,59},{64,6... | collective-permute-start | bytes 786440 | tf_op jit(solution)/shard_map/ppermute | solution.py:42
  130.6 9.8 %collective-permute-start.47 = (bf16[2,128,512]{2,1,0:T(8,128)(2,1)S(1)}, bf16[2,128,512]{2,1,0:T(8,128)(2,1)S(1)}, u32[]{:S(2)}, u32[]{:S(2)}) collective-permute-start(bf16[2,128,512]{2,1,0:T(8,128)(2,1)S(1)} %get-tuple-element.46), channel_id=1, source_target_pairs={{0,2},{8,10},{16,18},{24,26},{32,34},{40,42},{48,50},{56,58},{64,6... | collective-permute-start | bytes 786440 | tf_op jit(solution)/shard_map/ppermute | solution.py:42
  131.8 14.1 %collective-permute-start.48 = (bf16[2,128,512]{2,1,0:T(8,128)(2,1)S(1)}, bf16[2,128,512]{2,1,0:T(8,128)(2,1)S(1)}, u32[]{:S(2)}, u32[]{:S(2)}) collective-permute-start(bf16[2,128,512]{2,1,0:T(8,128)(2,1)S(1)} %get-tuple-element.47), channel_id=1, source_target_pairs={{0,1},{8,9},{16,17},{24,25},{32,33},{40,41},{48,49},{56,57},{64,65... | collective-permute-start | bytes 786440 | tf_op jit(solution)/shard_map/ppermute | solution.py:42
  131.9 17.1 %collective-permute-start.42 = (bf16[512,512]{1,0:T(8,128)(2,1)S(1)}, bf16[512,512]{1,0:T(8,128)(2,1)S(1)}, u32[]{:S(2)}, u32[]{:S(2)}) collective-permute-start(bf16[512,512]{1,0:T(8,128)(2,1)S(1)} %get-tuple-element.43), channel_id=1, source_target_pairs={{0,68},{8,76},{16,84},{24,92},{32,100},{40,108},{48,116},{56,124},... | collective-permute-start | bytes 1572872 | tf_op jit(solution)/shard_map/ppermute | solution.py:42
  146.1 5.9 %collective-permute-start.49 = (bf16[128,512]{1,0:T(8,128)(2,1)S(1)}, bf16[128,512]{1,0:T(8,128)(2,1)S(1)}, u32[]{:S(2)}, u32[]{:S(2)}) collective-permute-start(bf16[128,512]{1,0:T(8,128)(2,1)S(1)} %fusion.4), channel_id=1, source_target_pairs={{0,68},{8,76},{16,84},{24,92},{32,100},{40,108},{48,116},{56,124},... | collective-permute-start | bytes 393224 | tf_op jit(solution)/shard_map/ppermute | solution.py:42
  149.2 4.3 %collective-permute-start.43 = (bf16[128,512]{1,0:T(8,128)(2,1)S(1)}, bf16[128,512]{1,0:T(8,128)(2,1)S(1)}, u32[]{:S(2)}, u32[]{:S(2)}) collective-permute-start(bf16[128,512]{1,0:T(8,128)(2,1)S(1)} %get-tuple-element.54), channel_id=1, source_target_pairs={{0,3},{8,11},{16,19},{24,27},{32,35},{40,43},{48,51},{56,59},{64,6... | collective-permute-start | bytes 393224 | tf_op jit(solution)/shard_map/ppermute | solution.py:42
  149.2 5.5 %collective-permute-start.44 = (bf16[128,512]{1,0:T(8,128)(2,1)S(1)}, bf16[128,512]{1,0:T(8,128)(2,1)S(1)}, u32[]{:S(2)}, u32[]{:S(2)}) collective-permute-start(bf16[128,512]{1,0:T(8,128)(2,1)S(1)} %get-tuple-element.56), channel_id=1, source_target_pairs={{0,2},{8,10},{16,18},{24,26},{32,34},{40,42},{48,50},{56,58},{64,6... | collective-permute-start | bytes 393224 | tf_op jit(solution)/shard_map/ppermute | solution.py:42
  150.2 8.2 %collective-permute-start.45 = (bf16[128,512]{1,0:T(8,128)(2,1)S(1)}, bf16[128,512]{1,0:T(8,128)(2,1)S(1)}, u32[]{:S(2)}, u32[]{:S(2)}) collective-permute-start(bf16[128,512]{1,0:T(8,128)(2,1)S(1)} %get-tuple-element.55), channel_id=1, source_target_pairs={{0,1},{8,9},{16,17},{24,25},{32,33},{40,41},{48,49},{56,57},{64,65... | collective-permute-start | bytes 393224 | tf_op jit(solution)/shard_map/ppermute | solution.py:42
  158.6 6.7 %collective-permute-start.50 = (bf16[128,1024]{1,0:T(8,128)(2,1)S(1)}, bf16[128,1024]{1,0:T(8,128)(2,1)S(1)}, u32[]{:S(2)}, u32[]{:S(2)}) collective-permute-start(bf16[128,1024]{1,0:T(8,128)(2,1)S(1)} %reduce-precision_convert_fusion), channel_id=1, source_target_pairs={{0,64},{8,72},{16,80},{24,88},{32,96},{40,104},{48,112},{56,120},{... | collective-permute-start | bytes 786440 | tf_op jit(solution)/shard_map/ppermute | solution.py:42
  165.4 5.8 %collective-permute-start.51 = (bf16[128,1024]{1,0:T(8,128)(2,1)S(1)}, bf16[128,1024]{1,0:T(8,128)(2,1)S(1)}, u32[]{:S(2)}, u32[]{:S(2)}) collective-permute-start(bf16[128,1024]{1,0:T(8,128)(2,1)S(1)} %fusion.5), channel_id=1, source_target_pairs={{0,16},{8,24},{16,0},{24,8},{32,48},{40,56},{48,32},{56,40},{64,80... | collective-permute-start | bytes 786440 | tf_op jit(solution)/shard_map/ppermute | solution.py:42
  171.3 6.5 %collective-permute-start.52 = (bf16[128,1024]{1,0:T(8,128)(2,1)S(1)}, bf16[128,1024]{1,0:T(8,128)(2,1)S(1)}, u32[]{:S(2)}, u32[]{:S(2)}) collective-permute-start(bf16[128,1024]{1,0:T(8,128)(2,1)S(1)} %fusion), channel_id=1, source_target_pairs={{0,48},{8,56},{16,32},{24,40},{32,16},{40,24},{48,0},{56,8},{64,11... | collective-permute-start | bytes 786440 | tf_op jit(solution)/shard_map/ppermute | solution.py:42
  178.0 5.4 %collective-permute-start.53 = (bf16[128,1024]{1,0:T(8,128)(2,1)S(1)}, bf16[128,1024]{1,0:T(8,128)(2,1)S(1)}, u32[]{:S(2)}, u32[]{:S(2)}) collective-permute-start(bf16[128,1024]{1,0:T(8,128)(2,1)S(1)} %add_convert_fusion), channel_id=1, source_target_pairs={{0,8},{8,0},{16,24},{24,16},{32,40},{40,32},{48,56},{56,48},{64,72... | collective-permute-start | bytes 786440 | tf_op jit(solution)/shard_map/ppermute | solution.py:42
  (23 other events, 147.5 us)
